TPU v7x, 32 devices: a whole 2x2x4 slice. The times are simulated.
32 devices in a mesh: lang: 4 (over z), shard: 8 (over y, x, core).
Axes of the slice: x: 2, y: 2, z: 4, core: 2. Of those that a mesh axis runs over, the one named last changes fastest.
Arguments:
- memory: bfloat16 [32, 16, 4096], P(('lang', 'shard')), may hold values from -6 to 6
- lang_id: int32 [32], P(('lang', 'shard')), may hold values from 0 to 3, as said below
- src_len: int32 [32], P(('lang', 'shard')), may hold values from 4 to 16
- tgt_len: int32 [32], P(('lang', 'shard')), may hold values from 32 to 128
- queries: bfloat16 [4, 16, 128, 4096], P('lang', 'shard'), may hold values from -64 to 64
- key_weight: bfloat16 [4, 4096, 4096], P('lang', None, 'shard'), may hold values from -1 to 1
- value_weight: bfloat16 [4, 4096, 4096], P('lang', None, 'shard'), may hold values from -0.09375 to 0.09375
- grad_context: bfloat16 [4, 16, 128, 4096], P('lang', 'shard'), may hold values from -6 to 6
Outputs:
- context: bfloat16 [4, 16, 128, 4096], P('lang', 'shard')
- grad_queries: bfloat16 [4, 16, 128, 4096], P('lang', 'shard')
- grad_memory: bfloat16 [32, 16, 4096], P(('lang', 'shard'))
- grad_key_weight: bfloat16 [4, 4096, 4096], P('lang', None, 'shard')
- grad_value_weight: bfloat16 [4, 4096, 4096], P('lang', None, 'shard')
Inputs may be any that keep to these rules, and one draw needn't show every extreme that they name: `lang_id`: among the 4 sentences of one column b (indices a * 8 + b), no language is named more than 2 times, and in every column some language is named exactly 2 times.
All inputs are finite; a program needn't handle non-finite values.
Results may differ from a plain program's by a relative error of at most 0.025.
The roundings to bfloat16 on the way count: a program that leaves them out, or rounds other values in their place, can miss the bound.
Values may be sent and summed in bfloat16 or wider, within the bound.
A program may use at most 128 MiB of HBM per device.

v0:
```python
import jax
import jax.numpy as jnp
from jax import lax
from jax.sharding import PartitionSpec as P

HEAD = 128


masked_score = -1e30


def attend(queries, key_rows, value_rows, grad_ctx, src_slot, tgt_slot):
    scaling = queries.shape[-1] ** (-0.5)
    source_rows = key_rows.shape[1]
    target_rows = queries.shape[1]
    scores = (
        jnp.einsum("nqhe,nkhe->nhqk", queries, key_rows, preferred_element_type=jnp.float32)
        * scaling
    )
    key_valid = jnp.arange(source_rows)[None, :] < jnp.maximum(src_slot, 1)[:, None]
    scores = jnp.where(key_valid[:, None, None, :], scores, masked_score)
    row_max = jnp.max(scores, axis=-1, keepdims=True)
    shifted = jnp.exp(scores - row_max)
    attention = shifted / jnp.sum(shifted, axis=-1, keepdims=True)
    attention_bf = attention.astype(jnp.bfloat16)
    row_valid = (jnp.arange(target_rows)[None, :] < tgt_slot[:, None])[:, :, None, None]
    context = jnp.einsum(
        "nhqk,nkhe->nqhe", attention_bf, value_rows, preferred_element_type=jnp.float32
    )
    context = jnp.where(row_valid, context, 0.0).astype(jnp.bfloat16)
    grad_masked = jnp.where(row_valid, grad_ctx, jnp.zeros_like(grad_ctx))
    grad_values = jnp.einsum(
        "nhqk,nqhe->nkhe", attention_bf, grad_masked, preferred_element_type=jnp.float32
    ).astype(jnp.bfloat16)
    grad_attention = jnp.einsum(
        "nqhe,nkhe->nhqk", grad_masked, value_rows, preferred_element_type=jnp.float32
    )
    row_dot = jnp.sum(attention * grad_attention, axis=-1, keepdims=True)
    grad_scores = (attention * (grad_attention - row_dot)).astype(jnp.bfloat16)
    grad_queries = (
        jnp.einsum("nhqk,nkhe->nqhe", grad_scores, key_rows, preferred_element_type=jnp.float32)
        * scaling
    ).astype(jnp.bfloat16)
    grad_keys = (
        jnp.einsum("nhqk,nqhe->nkhe", grad_scores, queries, preferred_element_type=jnp.float32)
        * scaling
    ).astype(jnp.bfloat16)
    return (context, grad_queries, grad_keys, grad_values)


def local(memory, lang_id, src_len, tgt_len, queries, key_weight, value_weight, grad_context):
    lang_count = lax.axis_size("lang")
    shard_count = lax.axis_size("shard")
    lang_index = lax.axis_index("lang")
    column_mem, column_ids, column_src, column_tgt = (
        lax.all_gather(memory, "lang", axis=0, tiled=True),
        lax.all_gather(lang_id, "lang", axis=0, tiled=True),
        lax.all_gather(src_len, "lang", axis=0, tiled=True),
        lax.all_gather(tgt_len, "lang", axis=0, tiled=True),
    )
    slots_dev = queries.shape[1]
    target_rows = queries.shape[2]
    source_rows = memory.shape[1]
    model_width = memory.shape[2]
    head_cols = key_weight.shape[2]
    matching = column_ids[:, None] == column_ids[None, :]
    earlier = jnp.arange(lang_count)[None, :] < jnp.arange(lang_count)[:, None]
    position = jnp.sum(jnp.where(matching & earlier, 1, 0), axis=1).astype(jnp.int32)
    selected = (column_ids[None, :] == lang_index) & (
        position[None, :] == jnp.arange(slots_dev)[:, None]
    )
    routed = jnp.einsum(
        "rj,jsd->rsd", selected.astype(jnp.bfloat16), column_mem, preferred_element_type=jnp.float32
    ).astype(jnp.bfloat16)
    own_src = jnp.sum(jnp.where(selected, column_src[None, :], 0), axis=1).astype(jnp.int32)
    own_tgt = jnp.sum(jnp.where(selected, column_tgt[None, :], 0), axis=1).astype(jnp.int32)
    key_local = key_weight[0]
    value_local = value_weight[0]
    group_rows = lax.all_gather(routed, "shard", axis=0, tiled=True)
    flattened = group_rows.reshape(-1, model_width)
    key_part = jnp.dot(flattened, key_local, preferred_element_type=jnp.float32).astype(
        jnp.bfloat16
    )
    value_part = jnp.dot(flattened, value_local, preferred_element_type=jnp.float32).astype(
        jnp.bfloat16
    )
    joined = jnp.concatenate([key_part, value_part], axis=1)
    projected = joined.reshape(group_rows.shape[0], source_rows, 2 * head_cols)
    key_rows = projected[:, :, :head_cols]
    value_rows = projected[:, :, head_cols:]
    total_slots = key_rows.shape[0]
    local_heads = head_cols // HEAD
    src_all, tgt_all = (
        lax.all_gather(own_src, "shard", axis=0, tiled=True),
        lax.all_gather(own_tgt, "shard", axis=0, tiled=True),
    )
    query_split = queries[0].reshape(slots_dev, target_rows, shard_count, head_cols)
    grad_split = grad_context[0].reshape(slots_dev, target_rows, shard_count, head_cols)
    query_heads, grad_heads = (
        lax.all_to_all(query_split, "shard", split_axis=2, concat_axis=0, tiled=True),
        lax.all_to_all(grad_split, "shard", split_axis=2, concat_axis=0, tiled=True),
    )
    target_shape = (total_slots, target_rows, local_heads, HEAD)
    source_shape = (total_slots, source_rows, local_heads, HEAD)
    context_heads, grad_query_heads, grad_keys, grad_values = attend(
        query_heads.reshape(target_shape),
        key_rows.reshape(source_shape),
        value_rows.reshape(source_shape),
        grad_heads.reshape(target_shape),
        src_all,
        tgt_all,
    )
    outgoing = (
        context_heads.reshape(total_slots, target_rows, 1, head_cols),
        grad_query_heads.reshape(total_slots, target_rows, 1, head_cols),
    )
    context_slots, grad_query_slots = (
        lax.all_to_all(outgoing[0], "shard", split_axis=0, concat_axis=2, tiled=True),
        lax.all_to_all(outgoing[1], "shard", split_axis=0, concat_axis=2, tiled=True),
    )
    context = context_slots.reshape(1, slots_dev, target_rows, shard_count * head_cols)
    grad_queries = grad_query_slots.reshape(1, slots_dev, target_rows, shard_count * head_cols)
    grad_keys = grad_keys.reshape(total_slots, source_rows, head_cols)
    grad_values = grad_values.reshape(total_slots, source_rows, head_cols)
    key_part = grad_keys.reshape(-1, head_cols)
    value_part = grad_values.reshape(-1, head_cols)
    contract = (((1,), (1,)), ((), ()))
    summed = lax.dot_general(key_part, key_local, contract, preferred_element_type=jnp.float32)
    summed = summed + lax.dot_general(
        value_part, value_local, contract, preferred_element_type=jnp.float32
    )
    slot_grads = lax.psum_scatter(
        summed.reshape(lax.axis_size("shard") * slots_dev, source_rows, model_width).astype(
            jnp.bfloat16
        ),
        "shard",
        scatter_dimension=0,
        tiled=True,
    )
    transpose_contract = (((0,), (0,)), ((), ()))
    flattened = group_rows.reshape(-1, model_width)
    grad_key_local = lax.dot_general(
        flattened,
        grad_keys.reshape(-1, head_cols),
        transpose_contract,
        preferred_element_type=jnp.float32,
    )
    grad_value_local = lax.dot_general(
        flattened,
        grad_values.reshape(-1, head_cols),
        transpose_contract,
        preferred_element_type=jnp.float32,
    )
    returned = lax.all_gather(slot_grads, "lang", axis=0, tiled=True)
    own_index = lang_id[0] * slots_dev + position[lang_index]
    grad_memory = lax.dynamic_slice_in_dim(returned, own_index, 1, 0)
    return (
        context,
        grad_queries,
        grad_memory,
        grad_key_local.astype(jnp.bfloat16)[None],
        grad_value_local.astype(jnp.bfloat16)[None],
    )


def solution(mesh):
    return jax.shard_map(
        local,
        mesh=mesh,
        in_specs=(
            P(("lang", "shard"), None, None),
            P(("lang", "shard")),
            P(("lang", "shard")),
            P(("lang", "shard")),
            P("lang", "shard", None, None),
            P("lang", None, "shard"),
            P("lang", None, "shard"),
            P("lang", "shard", None, None),
        ),
        out_specs=(
            P("lang", "shard", None, None),
            P("lang", "shard", None, None),
            P(("lang", "shard"), None, None),
            P("lang", None, "shard"),
            P("lang", None, "shard"),
        ),
        check_vma=False,
    )
```

profile of v0, /device:TPU:0, one launch (start us, length us, event | category | flops | bytes accessed | tf_op | source)
XLA Modules:
  0.0 228.8 jit_solution(7422767592355214845)
XLA Ops:
  12.7 9.9 %all-reduce.6 = (s32[4]{0:T(128)S(1)}, s32[4]{0:T(128)S(1)}, s32[4]{0:T(128)S(1)}) all-reduce(s32[4]{0:T(128)S(1)} %dynamic-update-slice.3, s32[4]{0:T(128)S(1)} %dynamic-update-slice, s32[4]{0:T(128)S(1)} %dynamic-update-slice.1), channel_id=1, replica_groups=mesh['lang'=4,'shard'=8] {'lang'}, use_global_device_ids=true, to_apply=%add.3 | all-reduce | flops 12 | bytes 96
  22.7 15.8 %all_gather.27 = bf16[4,16,4096]{2,1,0:T(8,128)(2,1)S(1)} all-gather(bf16[1,16,4096]{2,1,0:T(8,128)(2,1)} %param.8), channel_id=1, replica_groups=mesh['lang'=4,'shard'=8] {'lang'}, dimensions={0}, use_global_device_ids=true | all-gather | bytes 655360 | tf_op jit(solution)/shard_map/all_gather | solution.py:56
  40.0 3.1 %copy.70 = bf16[1,2,128,4096]{2,3,1,0:T(8,128)(2,1)S(1)} copy(bf16[1,2,128,4096]{3,2,1,0:T(8,128)(2,1)} %param.12) | data formatting | bytes 4194304 | tf_op args[4]
  44.6 3.9 %all-to-all-start = ((bf16[2,128,8,512]{1,3,0,2:T(8,128)(2,1)}), bf16[2,128,8,512]{1,3,0,2:T(8,128)(2,1)S(1)}, u32[]{:S(2)}, u32[]{:S(2)}) async-start(bf16[2,128,8,512]{1,3,0,2:T(8,128)(2,1)} %copy.71), calls=%async_computation | async-start | bytes 4194304 | tf_op jit(solution)/shard_map/all_to_all | solution.py:100
  50.3 33.9 %all-reduce.5 = (s32[16]{0:T(128)S(1)}, s32[16]{0:T(128)S(1)}) all-reduce(s32[16]{0:T(128)S(1)} %dynamic-update-slice.2, s32[16]{0:T(128)S(1)} %dynamic-update-slice.4), channel_id=1, replica_groups=mesh['lang'=4,'shard'=8] {'shard'}, use_global_device_ids=true, to_apply=%add.2 | all-reduce | flops 32 | bytes 256
  84.2 4.1 %copy.77 = bf16[1,2,128,4096]{2,3,1,0:T(8,128)(2,1)} copy(bf16[1,2,128,4096]{3,2,1,0:T(8,128)(2,1)} %param.15) | data formatting | bytes 4194304 | tf_op args[7]
  88.2 3.1 %copy.78 = bf16[2,128,8,512]{1,3,0,2:T(8,128)(2,1)} copy(bf16[2,128,8,512]{1,3,2,0:T(8,128)(2,1)} %bitcast.119) | data formatting | bytes 4194304 | tf_op jit(solution)/shard_map/reshape;squeeze | solution.py:98
  91.3 4.4 %all-to-all-start.2 = ((bf16[2,128,8,512]{1,3,0,2:T(8,128)(2,1)}), bf16[2,128,8,512]{1,3,0,2:T(8,128)(2,1)}, u32[]{:S(2)}, u32[]{:S(2)}) async-start(bf16[2,128,8,512]{1,3,0,2:T(8,128)(2,1)} %copy.78), calls=%async_computation.2 | async-start | bytes 4194304 | tf_op jit(solution)/shard_map/all_to_all | solution.py:101
  95.9 4.2 %fusion.17 = bf16[256,512]{1,0:T(8,128)(2,1)S(1)} fusion(bf16[256,4096]{1,0:T(8,128)(2,1)} %bitcast.113, bf16[1,4096,512]{2,1,0:T(8,128)(2,1)} %param.13), kind=kOutput, calls=%fused_computation.26 | convolution fusion | flops 1073872896 | bytes 6553600 | tf_op jit(solution)/shard_map/dot_general | solution.py:81
  102.7 19.7 %all-to-all-done.2 = bf16[2,128,8,512]{1,3,0,2:T(8,128)(2,1)} async-done(((bf16[2,128,8,512]{1,3,0,2:T(8,128)(2,1)}), bf16[2,128,8,512]{1,3,0,2:T(8,128)(2,1)}, u32[]{:S(2)}, u32[]{:S(2)}) %all-to-all-start.2) | async-done | bytes 2097184 | tf_op jit(solution)/shard_map/all_to_all | solution.py:101
  122.4 2.8 %fusion.26 = bf16[16,16,4,128]{3,1,2,0:T(8,128)(2,1)S(1)} fusion(bf16[16,128,4,128]{1,3,2,0:T(8,128)(2,1)} %bitcast.20, pred[16,128]{1,0:T(8,128)(4,1)S(1)} %iota_compare_fusion.1, f32[16,4,128,16]{2,3,1,0:T(8,128)S(1)} %get-tuple-element.15, f32[16,4,128]{2,1,0:T(4,128)S(1)} %get-tuple-element.14), kind=kOutput, calls=%fused_computation.31 | convolution fusion | flops 34996224 | bytes 2918400 | tf_op jit(solution)/shard_map/nhqk,nqhe->nkhe/dot_general | solution.py:32
  131.8 2.6 %fusion.3 = bf16[256,4096]{1,0:T(8,128)(2,1)} fusion(f32[256,4096]{1,0:T(8,128)S(1)} %fusion.7, bf16[1,4096,512]{2,1,0:T(8,128)(2,1)S(1)} %copy-done.5, bf16[32,8,4,128]{3,2,1,0:T(4,128)(2,1)S(1)} %bitcast.123), kind=kOutput, calls=%fused_computation.6 | convolution fusion | flops 1075838976 | bytes 10747904 | tf_op jit(solution)/shard_map/dot_general | solution.py:129
  136.6 3.7 %all-to-all-start.3 = ((bf16[16,128,1,512]{1,3,2,0:T(8,128)(2,1)}), bf16[16,128,1,512]{1,3,2,0:T(8,128)(2,1)S(1)}, u32[]{:S(2)}, u32[]{:S(2)}) async-start(bf16[16,128,1,512]{1,3,2,0:T(8,128)(2,1)} %bitcast.23), calls=%async_computation.3 | async-start | bytes 4194304 | tf_op jit(solution)/shard_map/all_to_all | solution.py:119
  142.4 30.1 %all-to-all-done.3 = bf16[16,128,1,512]{1,3,2,0:T(8,128)(2,1)S(1)} async-done(((bf16[16,128,1,512]{1,3,2,0:T(8,128)(2,1)}), bf16[16,128,1,512]{1,3,2,0:T(8,128)(2,1)S(1)}, u32[]{:S(2)}, u32[]{:S(2)}) %all-to-all-start.3) | async-done | bytes 2097184 | tf_op jit(solution)/shard_map/all_to_all | solution.py:119
  173.8 4.7 %all-to-all-start.1 = ((bf16[16,128,1,512]{1,3,2,0:T(8,128)(2,1)}), bf16[16,128,1,512]{1,3,2,0:T(8,128)(2,1)}, u32[]{:S(2)}, u32[]{:S(2)}) async-start(bf16[16,128,1,512]{1,3,2,0:T(8,128)(2,1)} %bitcast.125), calls=%async_computation.1 | async-start | bytes 4194304 | tf_op jit(solution)/shard_map/all_to_all | solution.py:118
  178.5 6.8 %reduce-scatter.2.cloned.1.call-done = bf16[2,16,4096]{2,1,0:T(8,128)(2,1)} async-done(((bf16[16,16,4096]{2,1,0:T(8,128)(2,1)}), bf16[2,16,4096]{2,1,0:T(8,128)(2,1)}) %reduce-scatter.2.cloned.1.call-update) | async-done | bytes 262160 | tf_op jit(solution)/shard_map/reduce_scatter | solution.py:132
  186.6 3.3 %fusion.1 = bf16[1,4096,512]{2,1,0:T(8,128)(2,1)} fusion(bf16[256,4096]{1,0:T(8,128)(2,1)S(1)} %bitcast.115, bf16[32,8,4,128]{3,2,1,0:T(4,128)(2,1)S(1)} %bitcast.122), kind=kOutput, calls=%fused_computation.3 | convolution fusion | flops 1075838976 | bytes 6553600 | tf_op jit(solution)/shard_map/dot_general | solution.py:142
  189.9 3.3 %fusion.2 = bf16[1,4096,512]{2,1,0:T(8,128)(2,1)} fusion(bf16[256,4096]{1,0:T(8,128)(2,1)S(1)} %bitcast.116, bf16[32,8,4,128]{3,2,1,0:T(4,128)(2,1)S(1)} %bitcast.124), kind=kOutput, calls=%fused_computation.4 | convolution fusion | flops 1075838976 | bytes 6553600 | tf_op jit(solution)/shard_map/dot_general | solution.py:148
  193.2 3.4 %copy.83 = bf16[2,128,8,1,512]{4,2,1,0,3:T(8,128)(2,1)S(1)} copy(bf16[2,128,8,1,512]{1,4,0,2,3:T(8,128)(2,1)} %bitcast.117) | data formatting | bytes 4194304 | tf_op jit(solution)/shard_map/all_to_all | solution.py:119
  196.6 2.3 %reshape.107 = bf16[1,2,128,4096]{3,2,1,0:T(8,128)(2,1)} reshape(bf16[2,128,8,1,512]{4,2,1,0,3:T(8,128)(2,1)S(1)} %copy.83) | data formatting | bytes 4194304 | tf_op jit(solution)/shard_map/reshape | solution.py:122
  198.9 7.4 %all-to-all-done.1 = bf16[16,128,1,512]{1,3,2,0:T(8,128)(2,1)} async-done(((bf16[16,128,1,512]{1,3,2,0:T(8,128)(2,1)}), bf16[16,128,1,512]{1,3,2,0:T(8,128)(2,1)}, u32[]{:S(2)}, u32[]{:S(2)}) %all-to-all-start.1) | async-done | bytes 2097184 | tf_op jit(solution)/shard_map/all_to_all | solution.py:118
  206.4 3.4 %copy.76 = bf16[2,128,8,1,512]{4,2,1,0,3:T(8,128)(2,1)S(1)} copy(bf16[2,128,8,1,512]{1,4,0,2,3:T(8,128)(2,1)} %bitcast.16) | data formatting | bytes 4194304 | tf_op jit(solution)/shard_map/all_to_all | solution.py:118
  209.8 2.3 %reshape.104 = bf16[1,2,128,4096]{3,2,1,0:T(8,128)(2,1)} reshape(bf16[2,128,8,1,512]{4,2,1,0,3:T(8,128)(2,1)S(1)} %copy.76) | data formatting | bytes 4194304 | tf_op jit(solution)/shard_map/reshape | solution.py:121
  212.1 8.6 %all-gather.5.cloned.1.call-done = bf16[8,16,4096]{2,1,0:T(8,128)(2,1)} async-done(((bf16[2,16,4096]{2,1,0:T(8,128)(2,1)}), bf16[8,16,4096]{2,1,0:T(8,128)(2,1)}) %all-gather.5.cloned.1.call-update) | async-done | bytes 1048592 | tf_op jit(solution)/shard_map/all_gather | solution.py:154
  (61 shorter events, 24.9 us)
Async XLA Ops:
  7.2 88.7 %all-gather.3.cloned.1.call-start = ((), (), s32[]{:S(2)}) async-start(), calls=%async_computation.5 | async-start | bytes 2359296 | tf_op jit(solution)/shard_map/all_gather | solution.py:79
  44.6 3.9 %copy-start.8 = (u32[32]{0:T(128)S(1)}, u32[32]{0:T(128)}, u32[]{:S(2)}) copy-start(u32[32]{0:T(128)} %constant.49) | copy-start | bytes 388
  44.6 46.7 %all-to-all-start = ((bf16[2,128,8,512]{1,3,0,2:T(8,128)(2,1)}), bf16[2,128,8,512]{1,3,0,2:T(8,128)(2,1)S(1)}, u32[]{:S(2)}, u32[]{:S(2)}) async-start(bf16[2,128,8,512]{1,3,0,2:T(8,128)(2,1)} %copy.71), calls=%async_computation | async-start | bytes 4194304 | tf_op jit(solution)/shard_map/all_to_all | solution.py:100
  91.3 31.0 %all-to-all-start.2 = ((bf16[2,128,8,512]{1,3,0,2:T(8,128)(2,1)}), bf16[2,128,8,512]{1,3,0,2:T(8,128)(2,1)}, u32[]{:S(2)}, u32[]{:S(2)}) async-start(bf16[2,128,8,512]{1,3,0,2:T(8,128)(2,1)} %copy.78), calls=%async_computation.2 | async-start | bytes 4194304 | tf_op jit(solution)/shard_map/all_to_all | solution.py:101
  95.7 89.6 %reduce-scatter.2.cloned.1.call-start = ((), (), s32[]{:S(2)}) async-start(), calls=%async_computation.6 | async-start | bytes 2359296 | tf_op jit(solution)/shard_map/reduce_scatter | solution.py:132
  95.9 4.2 %copy-start = (bf16[16,16,4096]{2,1,0:T(8,128)(2,1)S(1)}, bf16[16,16,4096]{2,1,0:T(8,128)(2,1)}, u32[]{:S(2)}) copy-start(bf16[16,16,4096]{2,1,0:T(8,128)(2,1)} %all-gather.3.cloned.1.call-done) | copy-start | bytes 6291460
  95.9 4.7 %copy-start.4 = (bf16[1,4096,512]{2,1,0:T(8,128)(2,1)S(1)}, bf16[1,4096,512]{2,1,0:T(8,128)(2,1)}, u32[]{:S(2)}) copy-start(bf16[1,4096,512]{2,1,0:T(8,128)(2,1)} %param.14) | copy-start | bytes 12582916
  102.7 24.8 %copy-start.6 = (f32[16,4,128,16]{2,3,1,0:T(8,128)}, f32[16,4,128,16]{2,3,1,0:T(8,128)S(1)}, u32[]{:S(2)}) copy-start(f32[16,4,128,16]{2,3,1,0:T(8,128)S(1)} %get-tuple-element.15) | copy-start | bytes 1572868
  127.4 2.2 copy-start.3
  129.6 2.2 copy-start.5
  136.5 3.8 %copy-start.7 = (f32[16,4,128,16]{2,3,1,0:T(8,128)S(1)}, f32[16,4,128,16]{2,3,1,0:T(8,128)}, u32[]{:S(2)}) copy-start(f32[16,4,128,16]{2,3,1,0:T(8,128)} %copy-done.6) | copy-start | bytes 1572868
  136.6 35.9 %all-to-all-start.3 = ((bf16[16,128,1,512]{1,3,2,0:T(8,128)(2,1)}), bf16[16,128,1,512]{1,3,2,0:T(8,128)(2,1)S(1)}, u32[]{:S(2)}, u32[]{:S(2)}) async-start(bf16[16,128,1,512]{1,3,2,0:T(8,128)(2,1)} %bitcast.23), calls=%async_computation.3 | async-start | bytes 4194304 | tf_op jit(solution)/shard_map/all_to_all | solution.py:119
  172.5 1.3 copy-start.2
  173.8 12.8 %copy-start.1 = (bf16[16,16,4096]{2,1,0:T(8,128)(2,1)S(1)}, bf16[16,16,4096]{2,1,0:T(8,128)(2,1)}, u32[]{:S(2)}) copy-start(bf16[16,16,4096]{2,1,0:T(8,128)(2,1)} %all-gather.3.cloned.1.call-done) | copy-start | bytes 6291460
  173.8 32.6 %all-to-all-start.1 = ((bf16[16,128,1,512]{1,3,2,0:T(8,128)(2,1)}), bf16[16,128,1,512]{1,3,2,0:T(8,128)(2,1)}, u32[]{:S(2)}, u32[]{:S(2)}) async-start(bf16[16,128,1,512]{1,3,2,0:T(8,128)(2,1)} %bitcast.125), calls=%async_computation.1 | async-start | bytes 4194304 | tf_op jit(solution)/shard_map/all_to_all | solution.py:118
  178.5 42.2 %all-gather.5.cloned.1.call-start = ((), (), s32[]{:S(2)}) async-start(), calls=%async_computation.7 | async-start | bytes 1310720 | tf_op jit(solution)/shard_map/all_gather | solution.py:154
Sparse Core Ops, SparseCore 0:
  40.1 41.8 all-gather.2
  134.6 50.7 reduce-scatter.1
  187.0 33.6 all-gather.4
where the time goes:
time: 230 us; the launch traced here: 229 us
  waiting for transfers between devices  72.7 us (32%)
  blocking collectives  59.6 us (26%)
  local copies, waits for them, and re-layouts  34.3 us (15%)
  matrix products  27.6 us (12%)
  between operations  17.2 us (7%)
  starting transfers between devices  16.7 us (7%)
    unnamed x2, blocking collectives  43.7 us
    all_to_all x1, waiting for transfers between devices, local(): lax.all_to_all(outgoing[1], 'shard', split_axis=0, concat_axis=2, tiled=T...  30.1 us
    all_to_all x1, waiting for transfers between devices, local(): lax.all_to_all(grad_split, 'shard', split_axis=2, concat_axis=0, tiled=True)  19.7 us
    all_gather x1, blocking collectives, local(): lax.all_gather(memory, 'lang', axis=0, tiled=True)  15.8 us
    unnamed x33, local copies, waits for them, and re-layouts  15.1 us
    all_gather x1, waiting for transfers between devices, local(): returned = lax.all_gather(slot_grads, 'lang', axis=0, tiled=True)  8.62 us
    all_to_all x1, waiting for transfers between devices, local(): lax.all_to_all(outgoing[0], 'shard', split_axis=0, concat_axis=2, tiled=T...  7.44 us
    reduce_scatter x1, waiting for transfers between devices, local(): lax.psum_scatter(summed.reshape(lax.axis_size('shard') * slots_dev, sourc...  6.8 us
  transfers between devices with their start and end apart: 7, of which 5 were waited for; matrix products, arithmetic and copies ran while one was open for 18% of the time, Pallas kernels for 0%

commit v1 on v0

--- a/solution.py
+++ b/solution.py
@@ -90,40 +90,31 @@
     value_rows = projected[:, :, head_cols:]
     total_slots = key_rows.shape[0]
     local_heads = head_cols // HEAD
-    src_all, tgt_all = (
-        lax.all_gather(own_src, "shard", axis=0, tiled=True),
-        lax.all_gather(own_tgt, "shard", axis=0, tiled=True),
+    outgoing = projected.reshape(total_slots * source_rows, 1, 2 * head_cols)
+    arrived = lax.all_to_all(outgoing, "shard", split_axis=0, concat_axis=1, tiled=True)
+    arrived = arrived.reshape(slots_dev, source_rows, shard_count, 2 * head_cols)
+    target_shape = (slots_dev, target_rows, shard_count * local_heads, HEAD)
+    source_shape = (slots_dev, source_rows, shard_count * local_heads, HEAD)
+    context, grad_queries, grad_keys, grad_values = attend(
+        queries[0].reshape(target_shape),
+        arrived[..., :head_cols].reshape(source_shape),
+        arrived[..., head_cols:].reshape(source_shape),
+        grad_context[0].reshape(target_shape),
+        own_src,
+        own_tgt,
     )
-    query_split = queries[0].reshape(slots_dev, target_rows, shard_count, head_cols)
-    grad_split = grad_context[0].reshape(slots_dev, target_rows, shard_count, head_cols)
-    query_heads, grad_heads = (
-        lax.all_to_all(query_split, "shard", split_axis=2, concat_axis=0, tiled=True),
-        lax.all_to_all(grad_split, "shard", split_axis=2, concat_axis=0, tiled=True),
+    context = context.reshape(1, slots_dev, target_rows, shard_count * head_cols)
+    grad_queries = grad_queries.reshape(1, slots_dev, target_rows, shard_count * head_cols)
+    back_shape = (slots_dev * source_rows, shard_count, head_cols)
+    back = jnp.concatenate(
+        [grad_keys.reshape(back_shape), grad_values.reshape(back_shape)], axis=2
     )
-    target_shape = (total_slots, target_rows, local_heads, HEAD)
-    source_shape = (total_slots, source_rows, local_heads, HEAD)
-    context_heads, grad_query_heads, grad_keys, grad_values = attend(
-        query_heads.reshape(target_shape),
-        key_rows.reshape(source_shape),
-        value_rows.reshape(source_shape),
-        grad_heads.reshape(target_shape),
-        src_all,
-        tgt_all,
-    )
-    outgoing = (
-        context_heads.reshape(total_slots, target_rows, 1, head_cols),
-        grad_query_heads.reshape(total_slots, target_rows, 1, head_cols),
-    )
-    context_slots, grad_query_slots = (
-        lax.all_to_all(outgoing[0], "shard", split_axis=0, concat_axis=2, tiled=True),
-        lax.all_to_all(outgoing[1], "shard", split_axis=0, concat_axis=2, tiled=True),
-    )
-    context = context_slots.reshape(1, slots_dev, target_rows, shard_count * head_cols)
-    grad_queries = grad_query_slots.reshape(1, slots_dev, target_rows, shard_count * head_cols)
-    grad_keys = grad_keys.reshape(total_slots, source_rows, head_cols)
-    grad_values = grad_values.reshape(total_slots, source_rows, head_cols)
-    key_part = grad_keys.reshape(-1, head_cols)
-    value_part = grad_values.reshape(-1, head_cols)
+    back = lax.all_to_all(back, "shard", split_axis=1, concat_axis=0, tiled=True)
+    back = back.reshape(total_slots * source_rows, 2 * head_cols)
+    key_part = back[:, :head_cols]
+    value_part = back[:, head_cols:]
+    grad_keys = key_part
+    grad_values = value_part
     contract = (((1,), (1,)), ((), ()))
     summed = lax.dot_general(key_part, key_local, contract, preferred_element_type=jnp.float32)
     summed = summed + lax.dot_general(

time: 230 us -> 202 us (0.88)
  blocking collectives: 59.6 us -> 37.9 us
  starting transfers between devices: 16.7 us -> 4.27 us
  waiting for transfers between devices: 72.7 us -> 81.7 us
  local copies, waits for them, and re-layouts: 34.3 us -> 26.9 us
  matrix products: 27.6 us -> 32.3 us
    all_to_all x4 -> x1, waiting for transfers between devices: 57.2 us -> 4.18 us  [local(): lax.all_to_all(outgoing, 'shard', split_axis=0, concat_axis=1, tiled=True)]
    unnamed x2 -> x1, blocking collectives: 43.7 us -> 9.89 us
    reduce_scatter x1, waiting for transfers between devices: 6.8 us -> 40.4 us  [local(): lax.psum_scatter(summed.reshape(lax.axis_size('shard') * slots_dev, sourc...]
    all_gather x1, waiting for transfers between devices: 0.01 us -> 27.7 us  [local(): group_rows = lax.all_gather(routed, 'shard', axis=0, tiled=True)]
    all_to_all x4 -> x1, starting transfers between devices: 16.6 us -> 4.14 us  [local(): lax.all_to_all(outgoing, 'shard', split_axis=0, concat_axis=1, tiled=True)]
    all_to_all x0 -> x1, blocking collectives: none -> 12.2 us  [local(): lax.all_to_all(back, 'shard', split_axis=1, concat_axis=0, tiled=True)]
    unnamed x33 -> x36, local copies, waits for them, and re-layouts: 15.1 us -> 22.2 us
    all_to_all x2 -> x0, local copies, waits for them, and re-layouts: 6.71 us -> none  [the longest x1 3.36 us: local(): lax.all_to_all(outgoing[0], 'shard', split_axis=0, concat_axis=2, tiled=T...]
  transfers between devices with their start and end apart: 7 -> 4, of which waited for: 5 -> 4; matrix products, arithmetic and copies ran while one was open for 18% -> 13% of each run, Pallas kernels for 0% -> 0%
where the time goes in v1:
time: 202 us; the launch traced here: 201 us
  waiting for transfers between devices  81.7 us (40%)
  blocking collectives  37.9 us (19%)
  matrix products  32.3 us (16%)
  local copies, waits for them, and re-layouts  26.9 us (13%)
  between operations  16.6 us (8%)
  starting transfers between devices  4.27 us (2%)
    reduce_scatter x1, waiting for transfers between devices, local(): lax.psum_scatter(summed.reshape(lax.axis_size('shard') * slots_dev, sourc...  40.4 us
    all_gather x1, waiting for transfers between devices, local(): group_rows = lax.all_gather(routed, 'shard', axis=0, tiled=True)  27.7 us
    unnamed x36, local copies, waits for them, and re-layouts  22.2 us
    all_gather x1, blocking collectives, local(): lax.all_gather(memory, 'lang', axis=0, tiled=True)  15.8 us
    all_to_all x1, blocking collectives, local(): lax.all_to_all(back, 'shard', split_axis=1, concat_axis=0, tiled=True)  12.2 us
    unnamed x1, blocking collectives  9.89 us
    all_gather x1, waiting for transfers between devices, local(): returned = lax.all_gather(slot_grads, 'lang', axis=0, tiled=True)  9.31 us
    dot_general x1, matrix products, local(): jnp.dot(flattened, key_local, preferred_element_type=jnp.float32)  4.21 us
  transfers between devices with their start and end apart: 4, of which 4 were waited for; matrix products, arithmetic and copies ran while one was open for 13% of the time, Pallas kernels for 0%

profile of v1, /device:TPU:0, one launch (start us, length us, event | category | flops | bytes accessed | tf_op | source)
XLA Modules:
  0.0 201.4 jit_solution(14964721472622215962)
XLA Ops:
  12.7 9.9 %all-reduce.3 = (s32[4]{0:T(128)S(1)}, s32[4]{0:T(128)S(1)}, s32[4]{0:T(128)S(1)}) all-reduce(s32[4]{0:T(128)S(1)} %dynamic-update-slice.2, s32[4]{0:T(128)S(1)} %dynamic-update-slice, s32[4]{0:T(128)S(1)} %dynamic-update-slice.1), channel_id=1, replica_groups=mesh['lang'=4,'shard'=8] {'lang'}, use_global_device_ids=true, to_apply=%add.2 | all-reduce | flops 12 | bytes 96
  22.7 15.8 %all_gather.20 = bf16[4,16,4096]{2,1,0:T(8,128)(2,1)S(1)} all-gather(bf16[1,16,4096]{2,1,0:T(8,128)(2,1)} %param.8), channel_id=1, replica_groups=mesh['lang'=4,'shard'=8] {'lang'}, dimensions={0}, use_global_device_ids=true | all-gather | bytes 655360 | tf_op jit(solution)/shard_map/all_gather | solution.py:56
  40.1 27.7 %all-gather.3.cloned.1.call-done = bf16[16,16,4096]{2,1,0:T(8,128)(2,1)} async-done(((bf16[2,16,4096]{2,1,0:T(8,128)(2,1)}), bf16[16,16,4096]{2,1,0:T(8,128)(2,1)}) %all-gather.3.cloned.1.call-update) | async-done | bytes 2097168 | tf_op jit(solution)/shard_map/all_gather | solution.py:79
  67.9 4.2 %fusion.32 = bf16[256,512]{1,0:T(8,128)(2,1)S(1)} fusion(bf16[256,4096]{1,0:T(8,128)(2,1)} %bitcast.75, bf16[1,4096,512]{2,1,0:T(8,128)(2,1)} %param.13), kind=kOutput, calls=%fused_computation.31 | convolution fusion | flops 1073872896 | bytes 6553600 | tf_op jit(solution)/shard_map/dot_general | solution.py:81
  76.6 4.1 %all-to-all-start = ((bf16[8,2,16384]{2,1,0:T(2,128)(2,1)}), bf16[8,2,16384]{2,1,0:T(2,128)(2,1)}, u32[]{:S(2)}, u32[]{:S(2)}) async-start(bf16[8,2,16384]{2,1,0:T(2,128)(2,1)} %reshape.121), calls=%async_computation | async-start | bytes 1048576 | tf_op jit(solution)/shard_map/all_to_all | solution.py:94
  80.9 3.5 %copy.87 = bf16[32,8,32,128]{3,2,1,0:T(8,128)(2,1)} copy(bf16[32,8,32,128]{3,1,2,0:T(8,128)(2,1)} %bitcast.88) | data formatting | bytes 4194304
  84.4 1.8 copy.88
  86.4 4.2 %all-to-all-done = bf16[8,2,16384]{2,1,0:T(2,128)(2,1)} async-done(((bf16[8,2,16384]{2,1,0:T(2,128)(2,1)}), bf16[8,2,16384]{2,1,0:T(2,128)(2,1)}, u32[]{:S(2)}, u32[]{:S(2)}) %all-to-all-start) | async-done | bytes 524320 | tf_op jit(solution)/shard_map/all_to_all | solution.py:94
  90.5 2.2 %reshape.122 = bf16[256,1,1024]{2,1,0:T(2,128)(2,1)S(1)} reshape(bf16[8,2,16384]{2,1,0:T(2,128)(2,1)} %all-to-all-done) | data formatting | bytes 1048576
  93.3 2.8 %fusion.63 = (f32[2,32,128]{2,1,0:T(8,128)S(1)}, f32[2,32,128,16]{2,3,1,0:T(8,128)S(1)}) fusion(bf16[2,128,32,128]{3,2,1,0:T(8,128)(2,1)} %bitcast.79, pred[2,16]{1,0:T(4,128)(4,1)S(1)} %iota_compare_fusion.1, bf16[2,16,32,128]{3,2,1,0:T(8,128)(2,1)S(1)} %reshape.99), kind=kOutput, calls=%fused_computation.69 | convolution fusion | flops 34078736 | bytes 2916384 | tf_op jit(solution)/shard_map/sub | solution.py:23
  97.0 2.5 %fusion.44 = bf16[2,16,32,128]{3,1,2,0:T(8,128)(2,1)S(1)} fusion(bf16[2,128,32,128]{3,2,1,0:T(8,128)(2,1)} %bitcast.90, pred[2,128]{1,0:T(4,128)(4,1)S(1)} %iota_compare_fusion.2, f32[2,32,128,16]{2,3,1,0:T(8,128)S(1)} %get-tuple-element.38, f32[2,32,128]{2,1,0:T(8,128)S(1)} %get-tuple-element.37), kind=kOutput, calls=%fused_computation.35 | convolution fusion | flops 34996224 | bytes 2916608 | tf_op jit(solution)/shard_map/nhqk,nqhe->nkhe/dot_general | solution.py:32
  100.1 3.1 %multiply_reduce_fusion = (f32[2,32,128]{2,1,0:T(8,128)S(1)}, f32[2,32,128,16]{2,3,1,0:T(8,128)S(1)}) fusion(f32[2,32,128,16]{2,3,1,0:T(8,128)} %copy-done.5, f32[2,32,128]{2,1,0:T(8,128)S(1)} %get-tuple-element.37, bf16[2,16,32,128]{3,2,1,0:T(8,128)(2,1)S(1)} %reshape.98, bf16[2,128,32,128]{3,2,1,0:T(8,128)(2,1)} %bitcast.91, ...), kind=kOutput, calls=%fused_computation.41 | convolution fusion | flops 34988032 | bytes 3473664 | tf_op jit(solution)/shard_map/nqhe,nkhe->nhqk/dot_general | solution.py:35
  104.8 12.2 %all_to_all.30 = bf16[32,8,1024]{2,0,1:T(8,128)(2,1)S(1)} all-to-all(bf16[32,8,1024]{2,0,1:T(8,128)(2,1)S(1)} %copy.81), channel_id=1, replica_groups=mesh['lang'=4,'shard'=8] {'shard'}, dimensions={1} | all-to-all | bytes 1048576 | tf_op jit(solution)/shard_map/all_to_all | solution.py:112
  116.9 3.6 %fusion.7 = f32[256,4096]{1,0:T(8,128)S(1)} fusion(bf16[1,4096,512]{2,1,0:T(8,128)(2,1)} %param.13, bf16[256,1024]{1,0:T(8,128)(2,1)S(1)} %bitcast.83), kind=kOutput, calls=%fused_computation.11 | convolution fusion | flops 1073741824 | bytes 8650752 | tf_op jit(solution)/shard_map/dot_general | solution.py:119
  120.6 2.6 %fusion.3 = bf16[256,4096]{1,0:T(8,128)(2,1)} fusion(f32[256,4096]{1,0:T(8,128)S(1)} %fusion.7, bf16[1,4096,512]{2,1,0:T(8,128)(2,1)S(1)} %copy-done.3, bf16[256,1024]{1,0:T(8,128)(2,1)S(1)} %bitcast.84), kind=kOutput, calls=%fused_computation.6 | convolution fusion | flops 1075838976 | bytes 10747904 | tf_op jit(solution)/shard_map/dot_general | solution.py:120
  123.3 40.4 %reduce-scatter.2.cloned.1.call-done = bf16[2,16,4096]{2,1,0:T(8,128)(2,1)} async-done(((bf16[16,16,4096]{2,1,0:T(8,128)(2,1)}), bf16[2,16,4096]{2,1,0:T(8,128)(2,1)}) %reduce-scatter.2.cloned.1.call-update) | async-done | bytes 262160 | tf_op jit(solution)/shard_map/reduce_scatter | solution.py:123
  165.0 2.1 %multiply_convert_fusion = bf16[2,32,128,128]{3,2,1,0:T(8,128)(2,1)} fusion(bf16[2,32,128,16]{2,3,1,0:T(8,128)(2,1)S(1)} %multiply_convert_fusion.1, bf16[2,16,32,128]{3,2,1,0:T(8,128)(2,1)S(1)} %reshape.99), kind=kOutput, calls=%fused_computation.15 | convolution fusion | flops 35651584 | bytes 2621440 | tf_op jit(solution)/shard_map/nhqk,nkhe->nqhe/dot_general | solution.py:41
  167.1 4.1 %copy.83 = bf16[1,2,128,4096]{3,2,1,0:T(8,128)(2,1)} copy(bf16[1,2,128,4096]{2,3,1,0:T(8,128)(2,1)} %bitcast.81) | data formatting | bytes 4194304
  171.2 2.1 %select_convert_fusion = bf16[2,32,128,128]{3,2,1,0:T(8,128)(2,1)} fusion(pred[2,128]{1,0:T(4,128)(4,1)S(1)} %iota_compare_fusion.2, bf16[2,16,32,128]{3,2,1,0:T(8,128)(2,1)S(1)} %copy-done.9, f32[2,32,128,16]{2,3,1,0:T(8,128)S(1)} %copy-done.7, f32[2,32,128]{2,1,0:T(8,128)S(1)} %get-tuple-element.37), kind=kOutput, calls=%fused_computation.16 | convolution fusion | flops 35913728 | bytes 2916608 | tf_op jit(solution)/shard_map/nhqk,nkhe->nqhe/dot_general | solution.py:27
  173.3 4.1 %copy.82 = bf16[1,2,128,4096]{3,2,1,0:T(8,128)(2,1)} copy(bf16[1,2,128,4096]{2,3,1,0:T(8,128)(2,1)} %bitcast.92) | data formatting | bytes 4194304
  177.4 3.3 %fusion.1 = bf16[1,4096,512]{2,1,0:T(8,128)(2,1)} fusion(bf16[256,4096]{1,0:T(8,128)(2,1)S(1)} %bitcast.77, bf16[256,1024]{1,0:T(8,128)(2,1)S(1)} %bitcast.85), kind=kOutput, calls=%fused_computation.3 | convolution fusion | flops 1075838976 | bytes 6553600 | tf_op jit(solution)/shard_map/dot_general | solution.py:133
  180.7 3.3 %fusion.2 = bf16[1,4096,512]{2,1,0:T(8,128)(2,1)} fusion(bf16[256,4096]{1,0:T(8,128)(2,1)S(1)} %bitcast.78, bf16[256,1024]{1,0:T(8,128)(2,1)S(1)} %bitcast.86), kind=kOutput, calls=%fused_computation.4 | convolution fusion | flops 1075838976 | bytes 6553600 | tf_op jit(solution)/shard_map/dot_general | solution.py:139
  184.0 9.3 %all-gather.5.cloned.1.call-done = bf16[8,16,4096]{2,1,0:T(8,128)(2,1)} async-done(((bf16[2,16,4096]{2,1,0:T(8,128)(2,1)}), bf16[8,16,4096]{2,1,0:T(8,128)(2,1)}) %all-gather.5.cloned.1.call-update) | async-done | bytes 1048592 | tf_op jit(solution)/shard_map/all_gather | solution.py:145
  193.3 1.6 constant_dynamic-slice_fusion
  (61 shorter events, 14.1 us)
Async XLA Ops:
  7.2 60.7 %all-gather.3.cloned.1.call-start = ((), (), s32[]{:S(2)}) async-start(), calls=%async_computation.3 | async-start | bytes 2359296 | tf_op jit(solution)/shard_map/all_gather | solution.py:79
  67.9 4.2 %copy-start = (bf16[16,16,4096]{2,1,0:T(8,128)(2,1)S(1)}, bf16[16,16,4096]{2,1,0:T(8,128)(2,1)}, u32[]{:S(2)}) copy-start(bf16[16,16,4096]{2,1,0:T(8,128)(2,1)} %all-gather.3.cloned.1.call-done) | copy-start | bytes 6291460
  67.9 4.7 %copy-start.2 = (bf16[1,4096,512]{2,1,0:T(8,128)(2,1)S(1)}, bf16[1,4096,512]{2,1,0:T(8,128)(2,1)}, u32[]{:S(2)}) copy-start(bf16[1,4096,512]{2,1,0:T(8,128)(2,1)} %param.14) | copy-start | bytes 12582916
  76.6 13.9 %all-to-all-start = ((bf16[8,2,16384]{2,1,0:T(2,128)(2,1)}), bf16[8,2,16384]{2,1,0:T(2,128)(2,1)}, u32[]{:S(2)}, u32[]{:S(2)}) async-start(bf16[8,2,16384]{2,1,0:T(2,128)(2,1)} %reshape.121), calls=%async_computation | async-start | bytes 1048576 | tf_op jit(solution)/shard_map/all_to_all | solution.py:94
  80.8 82.9 %reduce-scatter.2.cloned.1.call-start = ((), (), s32[]{:S(2)}) async-start(), calls=%async_computation.4 | async-start | bytes 2359296 | tf_op jit(solution)/shard_map/reduce_scatter | solution.py:123
  80.8 3.6 %copy-start.4 = (bf16[1,2,128,4096]{3,2,1,0:T(8,128)(2,1)S(1)}, bf16[1,2,128,4096]{3,2,1,0:T(8,128)(2,1)}, u32[]{:S(2)}) copy-start(bf16[1,2,128,4096]{3,2,1,0:T(8,128)(2,1)} %param.15) | copy-start | bytes 6291460
  96.2 0.8 copy-start.5
  100.0 3.1 %copy-start.8 = (bf16[2,16,32,128]{3,2,1,0:T(8,128)(2,1)}, bf16[2,16,32,128]{3,2,1,0:T(8,128)(2,1)S(1)}, u32[]{:S(2)}) copy-start(bf16[2,16,32,128]{3,2,1,0:T(8,128)(2,1)S(1)} %reshape.98) | copy-start | bytes 786436
  100.0 3.1 %copy-start.6 = (f32[2,32,128,16]{2,3,1,0:T(8,128)S(1)}, f32[2,32,128,16]{2,3,1,0:T(8,128)}, u32[]{:S(2)}) copy-start(f32[2,32,128,16]{2,3,1,0:T(8,128)} %copy-done.5) | copy-start | bytes 1572868
  100.0 3.3 %copy-start.1 = (bf16[32,8,32,128]{3,2,1,0:T(8,128)(2,1)S(1)}, bf16[32,8,32,128]{3,2,1,0:T(8,128)(2,1)}, u32[]{:S(2)}) copy-start(bf16[32,8,32,128]{3,2,1,0:T(8,128)(2,1)} %copy.87) | copy-start | bytes 6291460
  116.9 3.6 %copy-start.3 = (bf16[1,4096,512]{2,1,0:T(8,128)(2,1)S(1)}, bf16[1,4096,512]{2,1,0:T(8,128)(2,1)}, u32[]{:S(2)}) copy-start(bf16[1,4096,512]{2,1,0:T(8,128)(2,1)} %param.14) | copy-start | bytes 12582916
  123.2 70.1 %all-gather.5.cloned.1.call-start = ((), (), s32[]{:S(2)}) async-start(), calls=%async_computation.5 | async-start | bytes 1310720 | tf_op jit(solution)/shard_map/all_gather | solution.py:145
  167.1 4.1 %copy-start.7 = (f32[2,32,128,16]{2,3,1,0:T(8,128)S(1)}, f32[2,32,128,16]{2,3,1,0:T(8,128)}, u32[]{:S(2)}) copy-start(f32[2,32,128,16]{2,3,1,0:T(8,128)} %copy-done.5) | copy-start | bytes 1572868
  167.1 4.2 %copy-start.9 = (bf16[2,16,32,128]{3,2,1,0:T(8,128)(2,1)S(1)}, bf16[2,16,32,128]{3,2,1,0:T(8,128)(2,1)}, u32[]{:S(2)}) copy-start(bf16[2,16,32,128]{3,2,1,0:T(8,128)(2,1)} %copy-done.8) | copy-start | bytes 786436
Sparse Core Ops, SparseCore 0:
  40.1 27.7 all-gather.2
  123.3 40.3 reduce-scatter.1
  165.4 27.9 all-gather.4

commit v2 on v1

v2 whole, which is shorter than its diff:
```python
import functools

import jax
import jax.numpy as jnp
from jax import lax
from jax.experimental import pallas as pl
from jax.experimental.pallas import tpu as pltpu
from jax.sharding import PartitionSpec as P

HEAD = 128
CHUNKS = 4
VMEM_BYTES = 50 * 1024 * 1024

masked_score = -1e30
MESH = pl.DeviceIdType.MESH
F32 = jnp.float32
BF16 = jnp.bfloat16


def remote(src, dst, send_sem, recv_sem, device):
    return pltpu.make_async_remote_copy(
        src_ref=src,
        dst_ref=dst,
        send_sem=send_sem,
        recv_sem=recv_sem,
        device_id=device,
        device_id_type=MESH,
    )


def enter(lang, shard, langs, shards):
    barrier = pltpu.get_barrier_semaphore()
    for step in range(1, langs):
        pl.semaphore_signal(
            barrier, inc=1, device_id=(lax.rem(lang + step, langs), shard), device_id_type=MESH
        )
    for step in range(1, shards):
        pl.semaphore_signal(
            barrier, inc=1, device_id=(lang, lax.rem(shard + step, shards)), device_id_type=MESH
        )
    pl.semaphore_wait(barrier, langs + shards - 2)


def selection(facts, lang, langs, slots):
    ids = [facts[j, 0:1, 0:1] for j in range(langs)]
    chosen = [[None] * langs for _ in range(slots)]
    for j in range(langs):
        rank = jnp.zeros((1, 1), jnp.int32)
        for k in range(j):
            rank = rank + jnp.where(ids[k] == ids[j], 1, 0)
        here = ids[j] == lang
        for r in range(slots):
            chosen[r][j] = jnp.where(here & (rank == r), 1, 0)
    return chosen


def route_kernel(
    langs, shards, slots,
    memory, facts_in, key_weight, value_weight,
    group, rows_out, facts, lengths,
    column, weights, total, outgoing,
    weight_sem, fact_send, fact_recv, z_send, z_recv,
    p_send, p_recv, s_send, s_recv, a_send, a_recv,
):
    lang = lax.axis_index("lang")
    shard = lax.axis_index("shard")
    core = lax.rem(shard, 2)
    chip = shard // 2
    chips = shards // 2
    sibling = (lang, chip * 2 + 1 - core)
    rows = memory.shape[0]
    width = memory.shape[1]
    cols = width // CHUNKS
    head_cols = key_weight.shape[1]
    block = slots * rows

    loads = [
        pltpu.make_async_copy(key_weight, weights.at[:, 0:head_cols], weight_sem.at[0]),
        pltpu.make_async_copy(
            value_weight, weights.at[:, head_cols : 2 * head_cols], weight_sem.at[1]
        ),
    ]
    for load in loads:
        load.start()
    enter(lang, shard, langs, shards)

    sent = []
    fact_copies = []
    for d in range(1, langs):
        copy = remote(
            facts_in, facts.at[lang], fact_send.at[d], fact_recv.at[d],
            (lax.rem(lang + d, langs), shard),
        )
        copy.start()
        fact_copies.append(copy)
    z_copies = []
    for c in range(CHUNKS):
        part = []
        for d in range(1, langs):
            copy = remote(
                memory.at[:, c * cols : (c + 1) * cols],
                column.at[lang, :, c * cols : (c + 1) * cols],
                z_send.at[d, c], z_recv.at[d, c],
                (lax.rem(lang + d, langs), shard),
            )
            copy.start()
            part.append(copy)
        z_copies.append(part)
    facts[lang] = facts_in[...]
    column[lang] = memory[...]
    for copy in fact_copies:
        copy.wait_recv()
    sent += fact_copies
    chosen = selection(facts, lang, langs, slots)
    for r in range(slots):
        for row, first in ((1, 0), (2, slots)):
            value = jnp.zeros((1, 1), jnp.int32)
            for j in range(langs):
                value = value + chosen[r][j] * facts[j, row : row + 1, 0:1]
            lengths[first + r : first + r + 1, :] = jnp.broadcast_to(value, (1, 128))
    weigh = [[chosen[r][j].astype(F32) for j in range(langs)] for r in range(slots)]

    def window(who, c):
        return group.at[pl.ds(pl.multiple_of(who * block, block), block), c * cols : (c + 1) * cols]

    p_copies = []
    s_copies = []
    for c in range(CHUNKS):
        for copy in z_copies[c]:
            copy.wait_recv()
        sent += z_copies[c]
        for r in range(slots):
            value = jnp.zeros((rows, cols), F32)
            for j in range(langs):
                value = value + column[j, :, c * cols : (c + 1) * cols].astype(F32) * weigh[r][j]
            start = pl.multiple_of(shard * block + r * rows, rows)
            group[pl.ds(start, rows), c * cols : (c + 1) * cols] = value.astype(BF16)
        part = []
        for d in range(1, chips):
            target = lax.rem(chip + d, chips) * 2 + core
            copy = remote(
                window(shard, c), window(shard, c), p_send.at[d, c], p_recv.at[d, c],
                (lang, target),
            )
            copy.start()
            part.append(copy)
        p_copies.append(part)
        copy = remote(window(shard, c), window(shard, c), s_send.at[0, c], s_recv.at[0, c], sibling)
        copy.start()
        s_copies.append([copy])
    for load in loads:
        load.wait()
    for c in range(CHUNKS):
        for d in range(1, chips):
            p_copies[c][d - 1].wait_recv()
            source = lax.rem(chip + chips - d, chips) * 2 + core
            copy = remote(
                window(source, c), window(source, c), s_send.at[d, c], s_recv.at[d, c], sibling
            )
            copy.start()
            s_copies[c].append(copy)
        sent += p_copies[c]
        for copy in s_copies[c]:
            copy.wait_recv()
        sent += s_copies[c]
        product = jnp.dot(
            group[:, c * cols : (c + 1) * cols],
            weights[c * cols : (c + 1) * cols, :],
            preferred_element_type=F32,
        )
        if c == 0:
            total[...] = product
        elif c < CHUNKS - 1:
            total[...] += product
        else:
            product = total[...] + product
            outgoing[...] = product.astype(BF16).reshape(outgoing.shape)
    exchange(lang, shard, shards, outgoing, rows_out, a_send, a_recv)
    for copy in sent:
        copy.wait_send()


def exchange(lang, shard, shards, outgoing, incoming, send_sem, recv_sem):
    copies = []
    for d in range(1, shards):
        target = lax.rem(shard + d, shards)
        copy = remote(
            outgoing.at[target], incoming.at[shard], send_sem.at[d], recv_sem.at[d], (lang, target)
        )
        copy.start()
        copies.append(copy)
    incoming[shard] = outgoing[shard]
    for copy in copies:
        copy.wait_recv()
    for copy in copies:
        copy.wait_send()


def attend_kernel(lengths, queries, grads, rows_in, context, grad_queries, grad_rows):
    slot = pl.program_id(0)
    groups = rows_in.shape[0]
    source_rows = rows_in.shape[1]
    head_cols = rows_in.shape[2] // 2
    target_rows = queries.shape[2]
    heads = head_cols // HEAD
    span = heads * source_rows
    scaling = HEAD ** (-0.5)
    slots = pl.num_programs(0)
    src = lengths[pl.ds(slot, 1), :]
    tgt = lengths[pl.ds(slots + slot, 1), :]
    src = jnp.maximum(src, 1)[:, 0:1].reshape(1, 1, 1)
    tgt = tgt[:, 0:1]
    key_valid = lax.broadcasted_iota(jnp.int32, (heads, source_rows, target_rows), 1) < src
    row_keep = lax.broadcasted_iota(jnp.int32, (target_rows, head_cols), 0) < tgt
    same = (
        lax.broadcasted_iota(jnp.int32, (span, head_cols), 0) // source_rows
        == lax.broadcasted_iota(jnp.int32, (span, head_cols), 1) // HEAD
    )

    def spread(rows):
        wide = jnp.concatenate([rows] * heads, axis=0) if heads > 1 else rows
        return jnp.where(same, wide.astype(F32), 0.0).astype(BF16)

    def gather(wide):
        return jnp.concatenate(
            [
                wide[h * source_rows : (h + 1) * source_rows, h * HEAD : (h + 1) * HEAD]
                for h in range(heads)
            ],
            axis=1,
        )

    nt = (((1,), (1,)), ((), ()))
    tn = (((0,), (0,)), ((), ()))
    for g in range(groups):
        lanes = slice(g * head_cols, (g + 1) * head_cols)
        q = queries[0, 0, :, lanes]
        grad = jnp.where(row_keep, grads[0, 0, :, lanes].astype(F32), 0.0).astype(BF16)
        keys = spread(rows_in[g, :, :head_cols])
        values = spread(rows_in[g, :, head_cols:])
        scores = lax.dot_general(keys, q, nt, preferred_element_type=F32) * scaling
        scores = scores.reshape(heads, source_rows, target_rows)
        scores = jnp.where(key_valid, scores, masked_score)
        shifted = jnp.exp(scores - jnp.max(scores, axis=1, keepdims=True))
        attention = shifted / jnp.sum(shifted, axis=1, keepdims=True)
        attention_bf = attention.reshape(span, target_rows).astype(BF16)
        out = lax.dot_general(attention_bf, values, tn, preferred_element_type=F32)
        context[0, 0, :, lanes] = jnp.where(row_keep, out, 0.0).astype(BF16)
        grad_values = jnp.dot(attention_bf, grad, preferred_element_type=F32)
        grad_attention = lax.dot_general(values, grad, nt, preferred_element_type=F32)
        grad_attention = grad_attention.reshape(heads, source_rows, target_rows)
        row_dot = jnp.sum(attention * grad_attention, axis=1, keepdims=True)
        grad_scores = attention * (grad_attention - row_dot)
        grad_scores = grad_scores.reshape(span, target_rows).astype(BF16)
        out = lax.dot_general(grad_scores, keys, tn, preferred_element_type=F32)
        grad_queries[0, 0, :, lanes] = (out * scaling).astype(BF16)
        grad_keys = jnp.dot(grad_scores, q, preferred_element_type=F32) * scaling
        grad_rows[g, :, :head_cols] = gather(grad_keys).astype(BF16)
        grad_rows[g, :, head_cols:] = gather(grad_values).astype(BF16)


def reduce_kernel(
    langs, shards, slots,
    grad_rows, facts, key_weight, value_weight,
    grad_memory, all_rows,
    weights, partial, first, paired, second, returning, third,
    weight_sem, a_send, a_recv, f_send, f_recv, p_send, p_recv, z_send, z_recv,
):
    lang = lax.axis_index("lang")
    shard = lax.axis_index("shard")
    core = lax.rem(shard, 2)
    chip = shard // 2
    chips = shards // 2
    sibling = (lang, chip * 2 + 1 - core)
    rows = grad_memory.shape[0]
    cols = grad_memory.shape[1] // CHUNKS
    head_cols = key_weight.shape[1]
    block = slots * rows
    nt = (((1,), (1,)), ((), ()))

    loads = [
        pltpu.make_async_copy(key_weight, weights.at[:, 0:head_cols], weight_sem.at[0]),
        pltpu.make_async_copy(
            value_weight, weights.at[:, head_cols : 2 * head_cols], weight_sem.at[1]
        ),
    ]
    for load in loads:
        load.start()
    enter(lang, shard, langs, shards)
    exchange(lang, shard, shards, grad_rows, all_rows, a_send, a_recv)
    for load in loads:
        load.wait()

    sent = []
    f_copies = []
    for c in range(CHUNKS):
        product = lax.dot_general(
            all_rows[...].reshape(shards * block, 2 * head_cols),
            weights[c * cols : (c + 1) * cols, :],
            nt,
            preferred_element_type=F32,
        )
        product = product.astype(BF16).reshape(chips, 2, block, cols)
        partial[c, 0] = product[:, 0]
        partial[c, 1] = product[:, 1]
        copy = remote(
            partial.at[c, 1 - core], first.at[c], f_send.at[c], f_recv.at[c], sibling
        )
        copy.start()
        f_copies.append(copy)
    p_copies = []
    for c in range(CHUNKS):
        f_copies[c].wait_recv()
        part = []
        for d in range(1, chips):
            other = lax.rem(chip + d, chips)
            pair = partial[c, core, other].astype(F32) + first[c, other].astype(F32)
            paired[c, d] = pair.astype(BF16)
            copy = remote(
                paired.at[c, d], second.at[c, d], p_send.at[c, d], p_recv.at[c, d],
                (lang, other * 2 + core),
            )
            copy.start()
            part.append(copy)
        p_copies.append(part)
    sent += f_copies
    chosen = selection(facts, lang, langs, slots)
    weigh = [[chosen[r][j].astype(F32) for j in range(langs)] for r in range(slots)]
    z_copies = []
    for c in range(CHUNKS):
        value = partial[c, core, chip].astype(F32) + first[c, chip].astype(F32)
        for d in range(1, chips):
            p_copies[c][d - 1].wait_recv()
            value = value + second[c, d].astype(F32)
        sent += p_copies[c]
        value = value.astype(BF16).astype(F32)
        for j in range(langs):
            back = value[0:rows] * weigh[0][j]
            for r in range(1, slots):
                back = back + value[r * rows : (r + 1) * rows] * weigh[r][j]
            returning[c, j] = back.astype(BF16)
        part = []
        for d in range(1, langs):
            other = lax.rem(lang + d, langs)
            copy = remote(
                returning.at[c, other], third.at[c, d], z_send.at[c, d], z_recv.at[c, d],
                (other, shard),
            )
            copy.start()
            part.append(copy)
        z_copies.append(part)
    for c in range(CHUNKS):
        value = returning[c, lang].astype(F32)
        for d in range(1, langs):
            z_copies[c][d - 1].wait_recv()
            value = value + third[c, d].astype(F32)
        sent += z_copies[c]
        grad_memory[:, c * cols : (c + 1) * cols] = value.astype(BF16)
    for copy in sent:
        copy.wait_send()


def local(memory, lang_id, src_len, tgt_len, queries, key_weight, value_weight, grad_context):
    langs = lax.axis_size("lang")
    shards = lax.axis_size("shard")
    chips = shards // 2
    slots = queries.shape[1]
    target_rows = queries.shape[2]
    rows = memory.shape[1]
    width = memory.shape[2]
    head_cols = key_weight.shape[2]
    cols = width // CHUNKS
    block = slots * rows
    total_rows = shards * block
    vmem = pl.BlockSpec(memory_space=pltpu.VMEM)
    hbm = pl.BlockSpec(memory_space=pl.ANY)
    dma = pltpu.SemaphoreType.DMA
    keys = key_weight[0]
    values = value_weight[0]
    facts_in = jnp.concatenate([lang_id, src_len, tgt_len, jnp.zeros((5,), jnp.int32)])
    facts_in = jnp.broadcast_to(facts_in[:, None], (8, 128))

    group, rows_in, facts, lengths = pl.pallas_call(
        functools.partial(route_kernel, langs, shards, slots),
        out_shape=(
            jax.ShapeDtypeStruct((total_rows, width), BF16),
            jax.ShapeDtypeStruct((shards, block, 2 * head_cols), BF16),
            jax.ShapeDtypeStruct((langs, 8, 128), jnp.int32),
            jax.ShapeDtypeStruct((2 * slots, 128), jnp.int32),
        ),
        in_specs=[vmem, vmem, hbm, hbm],
        out_specs=(vmem, vmem, vmem, vmem),
        scratch_shapes=[
            pltpu.VMEM((langs, rows, width), BF16),
            pltpu.VMEM((width, 2 * head_cols), BF16),
            pltpu.VMEM((total_rows, 2 * head_cols), F32),
            pltpu.VMEM((shards, block, 2 * head_cols), BF16),
            dma((2,)),
            dma((langs,)),
            dma((langs,)),
            dma((langs, CHUNKS)),
            dma((langs, CHUNKS)),
            dma((chips, CHUNKS)),
            dma((chips, CHUNKS)),
            dma((chips, CHUNKS)),
            dma((chips, CHUNKS)),
            dma((shards,)),
            dma((shards,)),
        ],
        compiler_params=pltpu.CompilerParams(
            collective_id=0, has_side_effects=True, vmem_limit_bytes=VMEM_BYTES
        ),
        name="route_and_project",
    )(memory[0], facts_in, keys, values)

    per_step = max(1, min(shards, 1024 // head_cols))
    steps = shards // per_step
    wide = pl.BlockSpec(
        (1, 1, target_rows, per_step * head_cols), lambda r, p: (0, r, 0, p)
    )
    narrow = pl.BlockSpec((per_step, rows, 2 * head_cols), lambda r, p: (p, r, 0))
    context, grad_queries, grad_rows = pl.pallas_call(
        attend_kernel,
        grid=(slots, steps),
        out_shape=(
            jax.ShapeDtypeStruct(queries.shape, BF16),
            jax.ShapeDtypeStruct(queries.shape, BF16),
            jax.ShapeDtypeStruct(rows_in.shape, BF16),
        ),
        in_specs=[
            pl.BlockSpec((2 * slots, 128), lambda r, p: (0, 0)), wide, wide, narrow
        ],
        out_specs=(wide, wide, narrow),
        compiler_params=pltpu.CompilerParams(vmem_limit_bytes=VMEM_BYTES),
        name="attend_both_ways",
    )(lengths, queries, grad_context, rows_in)

    grad_memory, all_rows = pl.pallas_call(
        functools.partial(reduce_kernel, langs, shards, slots),
        out_shape=(
            jax.ShapeDtypeStruct((rows, width), BF16),
            jax.ShapeDtypeStruct((shards, block, 2 * head_cols), BF16),
        ),
        in_specs=[vmem, vmem, hbm, hbm],
        out_specs=(vmem, vmem),
        scratch_shapes=[
            pltpu.VMEM((width, 2 * head_cols), BF16),
            pltpu.VMEM((CHUNKS, 2, chips, block, cols), BF16),
            pltpu.VMEM((CHUNKS, chips, block, cols), BF16),
            pltpu.VMEM((CHUNKS, chips, block, cols), BF16),
            pltpu.VMEM((CHUNKS, chips, block, cols), BF16),
            pltpu.VMEM((CHUNKS, langs, rows, cols), BF16),
            pltpu.VMEM((CHUNKS, langs, rows, cols), BF16),
            dma((2,)),
            dma((shards,)),
            dma((shards,)),
            dma((CHUNKS,)),
            dma((CHUNKS,)),
            dma((CHUNKS, chips)),
            dma((CHUNKS, chips)),
            dma((CHUNKS, langs)),
            dma((CHUNKS, langs)),
        ],
        compiler_params=pltpu.CompilerParams(
            collective_id=1, has_side_effects=True, vmem_limit_bytes=VMEM_BYTES
        ),
        name="reduce_and_return",
    )(grad_rows, facts, keys, values)

    flat = all_rows.reshape(total_rows, 2 * head_cols)
    tn = (((0,), (0,)), ((), ()))
    grad_key = lax.dot_general(group, flat[:, :head_cols], tn, preferred_element_type=F32)
    grad_value = lax.dot_general(group, flat[:, head_cols:], tn, preferred_element_type=F32)
    return (
        context,
        grad_queries,
        grad_memory[None],
        grad_key.astype(BF16)[None],
        grad_value.astype(BF16)[None],
    )


def solution(mesh):
    return jax.shard_map(
        local,
        mesh=mesh,
        in_specs=(
            P(("lang", "shard"), None, None),
            P(("lang", "shard")),
            P(("lang", "shard")),
            P(("lang", "shard")),
            P("lang", "shard", None, None),
            P("lang", None, "shard"),
            P("lang", None, "shard"),
            P("lang", "shard", None, None),
        ),
        out_specs=(
            P("lang", "shard", None, None),
            P("lang", "shard", None, None),
            P(("lang", "shard"), None, None),
            P("lang", None, "shard"),
            P("lang", None, "shard"),
        ),
        check_vma=False,
    )
```

time: 202 us -> 90.3 us (0.45)
  waiting for transfers between devices: 81.7 us -> 0 us
  Pallas kernels: 0 us -> 79.1 us
  blocking collectives: 37.9 us -> 0 us
  matrix products: 32.3 us -> 6.63 us
  local copies, waits for them, and re-layouts: 26.9 us -> 1.64 us
  between operations: 16.6 us -> 2.61 us
  starting transfers between devices: 4.27 us -> 0 us
    pallas_call x0 -> x3, Pallas kernels: none -> 79.1 us  [the longest x1 34.7 us: local(): pl.pallas_call(functools.partial(route_kernel, langs, shards, slots), out...]
    reduce_scatter x1 -> x0, waiting for transfers between devices: 40.4 us -> none  [local(): lax.psum_scatter(summed.reshape(lax.axis_size('shard') * slots_dev, sourc...]
    all_gather x2 -> x0, waiting for transfers between devices: 37.1 us -> none  [the longest x1 27.7 us: local(): group_rows = lax.all_gather(routed, 'shard', axis=0, tiled=True)]
    dot_general x12 -> x2, matrix products: 29.5 us -> 6.63 us  [the longest x1 3.32 us: local(): lax.dot_general(group, flat[:, :head_cols], tn, preferred_element_type=F32)]
    unnamed x36 -> x5, local copies, waits for them, and re-layouts: 22.2 us -> 1.56 us
    all_gather x1 -> x0, blocking collectives: 15.8 us -> none  [local(): lax.all_gather(memory, 'lang', axis=0, tiled=True)]
    all_to_all x1 -> x0, blocking collectives: 12.2 us -> none  [local(): lax.all_to_all(back, 'shard', split_axis=1, concat_axis=0, tiled=True)]
    unnamed x1 -> x0, blocking collectives: 9.89 us -> none
  transfers between devices with their start and end apart: 4 -> 0, of which waited for: 4 -> 0; matrix products, arithmetic and copies ran while one was open for 13% -> 0% of each run, Pallas kernels for 0% -> 0%
where the time goes in v2:
time: 90.3 us; the launch traced here: 90.1 us
  Pallas kernels  79.1 us (88%)
  matrix products  6.63 us (7%)
  between operations  2.61 us (3%)
  local copies, waits for them, and re-layouts  1.64 us (2%)
    pallas_call x1, Pallas kernels, local(): pl.pallas_call(functools.partial(route_kernel, langs, shards, slots), out...  34.7 us
    pallas_call x1, Pallas kernels, local(): pl.pallas_call(functools.partial(reduce_kernel, langs, shards, slots), ou...  32.5 us
    pallas_call x1, Pallas kernels, local(): pl.pallas_call(attend_kernel, grid=(slots, steps), out_shape=(jax.ShapeDt...  12 us
    dot_general x1, matrix products, local(): lax.dot_general(group, flat[:, :head_cols], tn, preferred_element_type=F32)  3.32 us
    dot_general x1, matrix products, local(): lax.dot_general(group, flat[:, head_cols:], tn, preferred_element_type=F32)  3.3 us

profile of v2, /device:TPU:0, one launch (start us, length us, event | category | flops | bytes accessed | tf_op | source)
XLA Modules:
  0.0 90.1 jit_solution(17130108951702858669)
XLA Ops:
  2.6 0.1 pad_add_fusion
  2.7 0.1 broadcast_in_dim.15.facts_in
  2.7 0.0 copy-start.1
  2.7 0.9 %copy-done.1 = bf16[1,16,4096]{2,1,0:T(8,128)(2,1)S(1)} copy-done((bf16[1,16,4096]{2,1,0:T(8,128)(2,1)S(1)}, bf16[1,16,4096]{2,1,0:T(8,128)(2,1)}, u32[]{:S(2)}) %copy-start.1) | copy-done | bytes 131096
  3.6 0.0 copy-start
  3.6 34.7 %route_and_project.1 = (bf16[256,4096]{1,0:T(8,128)(2,1)S(1)}, bf16[8,32,1024]{2,1,0:T(8,128)(2,1)S(1)}, s32[4,8,128]{2,1,0:T(8,128)S(1)}, s32[4,128]{1,0:T(4,128)S(1)}) custom-call(bf16[16,4096]{1,0:T(8,128)(2,1)S(1)} %bitcast.13, s32[8,128]{1,0:T(8,128)S(1)} %broadcast_in_dim.15.facts_in, bf16[4096,512]{1,0:T(8,128)(2,1)} %bitcast.15, ...), custom_call_target="tpu_custom_call" | custom-call | tf_op jit(solution)/shard_map/route_and_project/pallas_call | solution.py:383
  38.3 0.0 copy-done
  38.3 12.0 %attend_both_ways.1 = (bf16[1,2,128,4096]{3,2,1,0:T(8,128)(2,1)}, bf16[1,2,128,4096]{3,2,1,0:T(8,128)(2,1)}, bf16[8,32,1024]{2,1,0:T(8,128)(2,1)S(1)}) custom-call(s32[4,128]{1,0:T(4,128)S(1)} %get-tuple-element.14.lengths, bf16[1,2,128,4096]{3,2,1,0:T(8,128)(2,1)S(1)} %copy-done, bf16[1,2,128,4096]{3,2,1,0:T(8,128)(2,1)} %grads.1, ...), custom_call_target="tpu_custom_call" | custom-call | tf_op jit(solution)/shard_map/attend_both_ways/pallas_call | solution.py:422
  50.3 32.5 %reduce_and_return.1 = (bf16[16,4096]{1,0:T(8,128)(2,1)S(1)}, bf16[8,32,1024]{2,1,0:T(8,128)(2,1)S(1)}) custom-call(bf16[8,32,1024]{2,1,0:T(8,128)(2,1)S(1)} %get-tuple-element.18.grad_rows, s32[4,8,128]{2,1,0:T(8,128)S(1)} %get-tuple-element.19.facts, bf16[4096,512]{1,0:T(8,128)(2,1)} %bitcast.16, bf16[4096,512]{1,0:T(8,128)(2,1)} %bitcast.18), custom_call_target="tpu_custom_call" | custom-call | tf_op jit(solution)/shard_map/reduce_and_return/pallas_call | solution.py:438
  82.8 3.3 %fusion.1 = bf16[1,4096,512]{2,1,0:T(8,128)(2,1)} fusion(bf16[256,4096]{1,0:T(8,128)(2,1)S(1)} %get-tuple-element.21, bf16[256,1024]{1,0:T(8,128)(2,1)S(1)} %bitcast.11), kind=kOutput, calls=%fused_computation.3 | convolution fusion | flops 1075838976 | bytes 6553600 | tf_op jit(solution)/shard_map/dot_general | solution.py:473
  86.1 3.3 %fusion = bf16[1,4096,512]{2,1,0:T(8,128)(2,1)} fusion(bf16[256,4096]{1,0:T(8,128)(2,1)S(1)} %get-tuple-element.21, bf16[256,1024]{1,0:T(8,128)(2,1)S(1)} %bitcast.12), kind=kOutput, calls=%fused_computation.2 | convolution fusion | flops 1075838976 | bytes 6553600 | tf_op jit(solution)/shard_map/dot_general | solution.py:472
  89.4 0.7 copy.17
  (1 shorter events, 0.0 us)
Async XLA Ops:
  2.7 0.9 %copy-start.1 = (bf16[1,16,4096]{2,1,0:T(8,128)(2,1)S(1)}, bf16[1,16,4096]{2,1,0:T(8,128)(2,1)}, u32[]{:S(2)}) copy-start(bf16[1,16,4096]{2,1,0:T(8,128)(2,1)} %param.8) | copy-start | bytes 393220
  3.6 34.7 %copy-start = (bf16[1,2,128,4096]{3,2,1,0:T(8,128)(2,1)S(1)}, bf16[1,2,128,4096]{3,2,1,0:T(8,128)(2,1)}, u32[]{:S(2)}) copy-start(bf16[1,2,128,4096]{3,2,1,0:T(8,128)(2,1)} %queries.1) | copy-start | bytes 6291460

commit v3 on v2

--- a/solution.py
+++ b/solution.py
@@ -9,6 +9,7 @@
 
 HEAD = 128
 CHUNKS = 4
+AHEAD = 2
 VMEM_BYTES = 50 * 1024 * 1024
 
 masked_score = -1e30
@@ -94,7 +95,8 @@
         copy.start()
         fact_copies.append(copy)
     z_copies = []
-    for c in range(CHUNKS):
+
+    def start_z(c):
         part = []
         for d in range(1, langs):
             copy = remote(
@@ -106,6 +108,9 @@
             copy.start()
             part.append(copy)
         z_copies.append(part)
+
+    for c in range(min(AHEAD, CHUNKS)):
+        start_z(c)
     facts[lang] = facts_in[...]
     column[lang] = memory[...]
     for copy in fact_copies:
@@ -125,10 +130,13 @@
 
     p_copies = []
     s_copies = []
-    for c in range(CHUNKS):
+
+    def route(c):
         for copy in z_copies[c]:
             copy.wait_recv()
-        sent += z_copies[c]
+        sent.extend(z_copies[c])
+        if c + AHEAD < CHUNKS:
+            start_z(c + AHEAD)
         for r in range(slots):
             value = jnp.zeros((rows, cols), F32)
             for j in range(langs):
@@ -148,9 +156,8 @@
         copy = remote(window(shard, c), window(shard, c), s_send.at[0, c], s_recv.at[0, c], sibling)
         copy.start()
         s_copies.append([copy])
-    for load in loads:
-        load.wait()
-    for c in range(CHUNKS):
+
+    def forward(c):
         for d in range(1, chips):
             p_copies[c][d - 1].wait_recv()
             source = lax.rem(chip + chips - d, chips) * 2 + core
@@ -159,10 +166,12 @@
             )
             copy.start()
             s_copies[c].append(copy)
-        sent += p_copies[c]
+        sent.extend(p_copies[c])
+
+    def project(c):
         for copy in s_copies[c]:
             copy.wait_recv()
-        sent += s_copies[c]
+        sent.extend(s_copies[c])
         product = jnp.dot(
             group[:, c * cols : (c + 1) * cols],
             weights[c * cols : (c + 1) * cols, :],
@@ -175,6 +184,17 @@
         else:
             product = total[...] + product
             outgoing[...] = product.astype(BF16).reshape(outgoing.shape)
+
+    for turn in range(CHUNKS + 2):
+        if turn < CHUNKS:
+            route(turn)
+        if 0 <= turn - 1 < CHUNKS:
+            forward(turn - 1)
+        if turn == 2:
+            for load in loads:
+                load.wait()
+        if 0 <= turn - 2:
+            project(turn - 2)
     exchange(lang, shard, shards, outgoing, rows_out, a_send, a_recv)
     for copy in sent:
         copy.wait_send()
@@ -308,8 +328,13 @@
         )
         copy.start()
         f_copies.append(copy)
+        if c == min(1, CHUNKS - 1):
+            chosen = selection(facts, lang, langs, slots)
+            weigh = [[chosen[r][j].astype(F32) for j in range(langs)] for r in range(slots)]
     p_copies = []
-    for c in range(CHUNKS):
+    z_copies = []
+
+    def send_pairs(c):
         f_copies[c].wait_recv()
         part = []
         for d in range(1, chips):
@@ -323,16 +348,12 @@
             copy.start()
             part.append(copy)
         p_copies.append(part)
-    sent += f_copies
-    chosen = selection(facts, lang, langs, slots)
-    weigh = [[chosen[r][j].astype(F32) for j in range(langs)] for r in range(slots)]
-    z_copies = []
-    for c in range(CHUNKS):
+
+    def send_back(c):
         value = partial[c, core, chip].astype(F32) + first[c, chip].astype(F32)
         for d in range(1, chips):
             p_copies[c][d - 1].wait_recv()
             value = value + second[c, d].astype(F32)
-        sent += p_copies[c]
         value = value.astype(BF16).astype(F32)
         for j in range(langs):
             back = value[0:rows] * weigh[0][j]
@@ -349,13 +370,24 @@
             copy.start()
             part.append(copy)
         z_copies.append(part)
-    for c in range(CHUNKS):
+
+    def finish(c):
         value = returning[c, lang].astype(F32)
         for d in range(1, langs):
             z_copies[c][d - 1].wait_recv()
             value = value + third[c, d].astype(F32)
-        sent += z_copies[c]
         grad_memory[:, c * cols : (c + 1) * cols] = value.astype(BF16)
+
+    for turn in range(CHUNKS + 1):
+        if turn < CHUNKS:
+            send_pairs(turn)
+        if 0 <= turn - 1:
+            send_back(turn - 1)
+    for c in range(CHUNKS):
+        finish(c)
+    sent += f_copies
+    for c in range(CHUNKS):
+        sent += p_copies[c] + z_copies[c]
     for copy in sent:
         copy.wait_send()
 

time: 90.3 us -> 89.5 us (level)
    pallas_call x1, Pallas kernels: 34.7 us -> 33.7 us  [local(): pl.pallas_call(functools.partial(route_kernel, langs, shards, slots), out...]
where the time goes in v3:
time: 89.5 us; the launch traced here: 89.4 us
  Pallas kernels  78.4 us (88%)
  matrix products  6.63 us (7%)
  between operations  2.61 us (3%)
  local copies, waits for them, and re-layouts  1.64 us (2%)
    pallas_call x1, Pallas kernels, local(): pl.pallas_call(functools.partial(route_kernel, langs, shards, slots), out...  33.7 us
    pallas_call x1, Pallas kernels, local(): pl.pallas_call(functools.partial(reduce_kernel, langs, shards, slots), ou...  32.7 us
    pallas_call x1, Pallas kernels, local(): pl.pallas_call(attend_kernel, grid=(slots, steps), out_shape=(jax.ShapeDt...  12 us
    dot_general x1, matrix products, local(): lax.dot_general(group, flat[:, :head_cols], tn, preferred_element_type=F32)  3.32 us
    dot_general x1, matrix products, local(): lax.dot_general(group, flat[:, head_cols:], tn, preferred_element_type=F32)  3.3 us

profile of v3, /device:TPU:0, one launch (start us, length us, event | category | flops | bytes accessed | tf_op | source)
XLA Modules:
  0.0 89.4 jit_solution(13246017465080075855)
XLA Ops:
  2.6 0.1 pad_add_fusion
  2.7 0.1 broadcast_in_dim.15.facts_in
  2.7 0.0 copy-start.1
  2.7 0.9 %copy-done.1 = bf16[1,16,4096]{2,1,0:T(8,128)(2,1)S(1)} copy-done((bf16[1,16,4096]{2,1,0:T(8,128)(2,1)S(1)}, bf16[1,16,4096]{2,1,0:T(8,128)(2,1)}, u32[]{:S(2)}) %copy-start.1) | copy-done | bytes 131096
  3.6 0.0 copy-start
  3.6 33.7 %route_and_project.1 = (bf16[256,4096]{1,0:T(8,128)(2,1)S(1)}, bf16[8,32,1024]{2,1,0:T(8,128)(2,1)S(1)}, s32[4,8,128]{2,1,0:T(8,128)S(1)}, s32[4,128]{1,0:T(4,128)S(1)}) custom-call(bf16[16,4096]{1,0:T(8,128)(2,1)S(1)} %bitcast.13, s32[8,128]{1,0:T(8,128)S(1)} %broadcast_in_dim.15.facts_in, bf16[4096,512]{1,0:T(8,128)(2,1)} %bitcast.15, ...), custom_call_target="tpu_custom_call" | custom-call | tf_op jit(solution)/shard_map/route_and_project/pallas_call | solution.py:415
  37.4 0.0 copy-done
  37.4 12.0 %attend_both_ways.1 = (bf16[1,2,128,4096]{3,2,1,0:T(8,128)(2,1)}, bf16[1,2,128,4096]{3,2,1,0:T(8,128)(2,1)}, bf16[8,32,1024]{2,1,0:T(8,128)(2,1)S(1)}) custom-call(s32[4,128]{1,0:T(4,128)S(1)} %get-tuple-element.14.lengths, bf16[1,2,128,4096]{3,2,1,0:T(8,128)(2,1)S(1)} %copy-done, bf16[1,2,128,4096]{3,2,1,0:T(8,128)(2,1)} %grads.1, ...), custom_call_target="tpu_custom_call" | custom-call | tf_op jit(solution)/shard_map/attend_both_ways/pallas_call | solution.py:454
  49.4 32.7 %reduce_and_return.1 = (bf16[16,4096]{1,0:T(8,128)(2,1)S(1)}, bf16[8,32,1024]{2,1,0:T(8,128)(2,1)S(1)}) custom-call(bf16[8,32,1024]{2,1,0:T(8,128)(2,1)S(1)} %get-tuple-element.18.grad_rows, s32[4,8,128]{2,1,0:T(8,128)S(1)} %get-tuple-element.19.facts, bf16[4096,512]{1,0:T(8,128)(2,1)} %bitcast.16, bf16[4096,512]{1,0:T(8,128)(2,1)} %bitcast.18), custom_call_target="tpu_custom_call" | custom-call | tf_op jit(solution)/shard_map/reduce_and_return/pallas_call | solution.py:470
  82.1 3.3 %fusion.1 = bf16[1,4096,512]{2,1,0:T(8,128)(2,1)} fusion(bf16[256,4096]{1,0:T(8,128)(2,1)S(1)} %get-tuple-element.21, bf16[256,1024]{1,0:T(8,128)(2,1)S(1)} %bitcast.11), kind=kOutput, calls=%fused_computation.3 | convolution fusion | flops 1075838976 | bytes 6553600 | tf_op jit(solution)/shard_map/dot_general | solution.py:505
  85.4 3.3 %fusion = bf16[1,4096,512]{2,1,0:T(8,128)(2,1)} fusion(bf16[256,4096]{1,0:T(8,128)(2,1)S(1)} %get-tuple-element.21, bf16[256,1024]{1,0:T(8,128)(2,1)S(1)} %bitcast.12), kind=kOutput, calls=%fused_computation.2 | convolution fusion | flops 1075838976 | bytes 6553600 | tf_op jit(solution)/shard_map/dot_general | solution.py:504
  88.7 0.7 copy.17
  (1 shorter events, 0.0 us)
Async XLA Ops:
  2.7 0.9 %copy-start.1 = (bf16[1,16,4096]{2,1,0:T(8,128)(2,1)S(1)}, bf16[1,16,4096]{2,1,0:T(8,128)(2,1)}, u32[]{:S(2)}) copy-start(bf16[1,16,4096]{2,1,0:T(8,128)(2,1)} %param.8) | copy-start | bytes 393220
  3.6 33.7 %copy-start = (bf16[1,2,128,4096]{3,2,1,0:T(8,128)(2,1)S(1)}, bf16[1,2,128,4096]{3,2,1,0:T(8,128)(2,1)}, u32[]{:S(2)}) copy-start(bf16[1,2,128,4096]{3,2,1,0:T(8,128)(2,1)} %queries.1) | copy-start | bytes 6291460

commit v4 on v3

--- a/solution.py
+++ b/solution.py
@@ -112,7 +112,9 @@
     for c in range(min(AHEAD, CHUNKS)):
         start_z(c)
     facts[lang] = facts_in[...]
-    column[lang] = memory[...]
+    own = pltpu.make_async_copy(memory, column.at[lang], weight_sem.at[2])
+    own.start()
+    own.wait()
     for copy in fact_copies:
         copy.wait_recv()
     sent += fact_copies
@@ -313,7 +315,10 @@
 
     sent = []
     f_copies = []
-    for c in range(CHUNKS):
+    chosen = selection(facts, lang, langs, slots)
+    weigh = [[chosen[r][j].astype(F32) for j in range(langs)] for r in range(slots)]
+
+    def project_back(c):
         product = lax.dot_general(
             all_rows[...].reshape(shards * block, 2 * head_cols),
             weights[c * cols : (c + 1) * cols, :],
@@ -328,9 +333,7 @@
         )
         copy.start()
         f_copies.append(copy)
-        if c == min(1, CHUNKS - 1):
-            chosen = selection(facts, lang, langs, slots)
-            weigh = [[chosen[r][j].astype(F32) for j in range(langs)] for r in range(slots)]
+
     p_copies = []
     z_copies = []
 
@@ -378,11 +381,13 @@
             value = value + third[c, d].astype(F32)
         grad_memory[:, c * cols : (c + 1) * cols] = value.astype(BF16)
 
-    for turn in range(CHUNKS + 1):
+    for turn in range(CHUNKS + 2):
         if turn < CHUNKS:
-            send_pairs(turn)
-        if 0 <= turn - 1:
-            send_back(turn - 1)
+            project_back(turn)
+        if 0 <= turn - 1 < CHUNKS:
+            send_pairs(turn - 1)
+        if 0 <= turn - 2:
+            send_back(turn - 2)
     for c in range(CHUNKS):
         finish(c)
     sent += f_copies
@@ -390,6 +395,15 @@
         sent += p_copies[c] + z_copies[c]
     for copy in sent:
         copy.wait_send()
+
+
+def weight_kernel(group, grads, grad_key, grad_value):
+    head_cols = grad_key.shape[2]
+    product = lax.dot_general(
+        group[...], grads[...], (((0,), (0,)), ((), ())), preferred_element_type=F32
+    )
+    grad_key[0] = product[:, :head_cols].astype(BF16)
+    grad_value[0] = product[:, head_cols:].astype(BF16)
 
 
 def local(memory, lang_id, src_len, tgt_len, queries, key_weight, value_weight, grad_context):
@@ -420,14 +434,14 @@
             jax.ShapeDtypeStruct((langs, 8, 128), jnp.int32),
             jax.ShapeDtypeStruct((2 * slots, 128), jnp.int32),
         ),
-        in_specs=[vmem, vmem, hbm, hbm],
+        in_specs=[hbm, vmem, hbm, hbm],
         out_specs=(vmem, vmem, vmem, vmem),
         scratch_shapes=[
             pltpu.VMEM((langs, rows, width), BF16),
             pltpu.VMEM((width, 2 * head_cols), BF16),
             pltpu.VMEM((total_rows, 2 * head_cols), F32),
             pltpu.VMEM((shards, block, 2 * head_cols), BF16),
-            dma((2,)),
+            dma((3,)),
             dma((langs,)),
             dma((langs,)),
             dma((langs, CHUNKS)),
@@ -445,7 +459,7 @@
         name="route_and_project",
     )(memory[0], facts_in, keys, values)
 
-    per_step = max(1, min(shards, 1024 // head_cols))
+    per_step = max(1, min(shards, 2048 // head_cols))
     steps = shards // per_step
     wide = pl.BlockSpec(
         (1, 1, target_rows, per_step * head_cols), lambda r, p: (0, r, 0, p)
@@ -500,15 +514,29 @@
     )(grad_rows, facts, keys, values)
 
     flat = all_rows.reshape(total_rows, 2 * head_cols)
-    tn = (((0,), (0,)), ((), ()))
-    grad_key = lax.dot_general(group, flat[:, :head_cols], tn, preferred_element_type=F32)
-    grad_value = lax.dot_general(group, flat[:, head_cols:], tn, preferred_element_type=F32)
+    tile = width // 8
+    out_tile = pl.BlockSpec((1, tile, head_cols), lambda i: (0, i, 0))
+    grad_key, grad_value = pl.pallas_call(
+        weight_kernel,
+        grid=(8,),
+        out_shape=(
+            jax.ShapeDtypeStruct(key_weight.shape, BF16),
+            jax.ShapeDtypeStruct(value_weight.shape, BF16),
+        ),
+        in_specs=[
+            pl.BlockSpec((total_rows, tile), lambda i: (0, i)),
+            pl.BlockSpec((total_rows, 2 * head_cols), lambda i: (0, 0)),
+        ],
+        out_specs=(out_tile, out_tile),
+        compiler_params=pltpu.CompilerParams(vmem_limit_bytes=VMEM_BYTES),
+        name="weight_gradients",
+    )(group, flat)
     return (
         context,
         grad_queries,
         grad_memory[None],
-        grad_key.astype(BF16)[None],
-        grad_value.astype(BF16)[None],
+        grad_key,
+        grad_value,
     )
 
 

time: 89.5 us -> 85.9 us (0.960)
  matrix products: 6.63 us -> 0 us
  Pallas kernels: 78.4 us -> 81.4 us
    dot_general x2 -> x0, matrix products: 6.63 us -> none  [the longest x1 3.32 us: local(): lax.dot_general(group, flat[:, :head_cols], tn, preferred_element_type=F32)]
    pallas_call x0 -> x1, Pallas kernels: none -> 5.73 us  [local(): pl.pallas_call(weight_kernel, grid=(8,), out_shape=(jax.ShapeDtypeStruct(...]
    pallas_call x1, Pallas kernels: 12 us -> 10.5 us  [local(): pl.pallas_call(attend_kernel, grid=(slots, steps), out_shape=(jax.ShapeDt...]
    pallas_call x1, Pallas kernels: 32.7 us -> 31.4 us  [local(): pl.pallas_call(functools.partial(reduce_kernel, langs, shards, slots), ou...]
where the time goes in v4:
time: 85.9 us; the launch traced here: 85.7 us
  Pallas kernels  81.4 us (95%)
  between operations  2.6 us (3%)
  local copies, waits for them, and re-layouts  1.64 us (2%)
    pallas_call x1, Pallas kernels, local(): pl.pallas_call(functools.partial(route_kernel, langs, shards, slots), out...  33.7 us
    pallas_call x1, Pallas kernels, local(): pl.pallas_call(functools.partial(reduce_kernel, langs, shards, slots), ou...  31.4 us
    pallas_call x1, Pallas kernels, local(): pl.pallas_call(attend_kernel, grid=(slots, steps), out_shape=(jax.ShapeDt...  10.5 us
    pallas_call x1, Pallas kernels, local(): pl.pallas_call(weight_kernel, grid=(8,), out_shape=(jax.ShapeDtypeStruct(...  5.73 us

profile of v4, /device:TPU:0, one launch (start us, length us, event | category | flops | bytes accessed | tf_op | source)
XLA Modules:
  0.0 85.7 jit_solution(8584481615680712921)
XLA Ops:
  2.6 0.1 pad_add_fusion
  2.7 0.1 broadcast_in_dim.4.facts_in
  2.7 0.0 copy-start.1
  2.7 0.9 %copy-done.1 = bf16[1,16,4096]{2,1,0:T(8,128)(2,1)S(1)} copy-done((bf16[1,16,4096]{2,1,0:T(8,128)(2,1)S(1)}, bf16[1,16,4096]{2,1,0:T(8,128)(2,1)}, u32[]{:S(2)}) %copy-start.1) | copy-done | bytes 131096
  3.6 0.0 copy-start
  3.6 33.7 %route_and_project.1 = (bf16[256,4096]{1,0:T(8,128)(2,1)S(1)}, bf16[8,32,1024]{2,1,0:T(8,128)(2,1)S(1)}, s32[4,8,128]{2,1,0:T(8,128)S(1)}, s32[4,128]{1,0:T(4,128)S(1)}) custom-call(bf16[16,4096]{1,0:T(8,128)(2,1)S(1)} %bitcast.6, s32[8,128]{1,0:T(8,128)S(1)} %broadcast_in_dim.4.facts_in, bf16[4096,512]{1,0:T(8,128)(2,1)} %bitcast.8, bf16[4096,512]{1,0:T(8,128)(2,1)} %bitcast.10), custom_call_target="tpu_custom_call" | custom-call | tf_op jit(solution)/shard_map/route_and_project/pallas_call | solution.py:429
  37.4 0.0 copy-done
  37.4 10.5 %attend_both_ways.1 = (bf16[1,2,128,4096]{3,2,1,0:T(8,128)(2,1)}, bf16[1,2,128,4096]{3,2,1,0:T(8,128)(2,1)}, bf16[8,32,1024]{2,1,0:T(8,128)(2,1)S(1)}) custom-call(s32[4,128]{1,0:T(4,128)S(1)} %get-tuple-element.16.lengths, bf16[1,2,128,4096]{3,2,1,0:T(8,128)(2,1)S(1)} %copy-done, bf16[1,2,128,4096]{3,2,1,0:T(8,128)(2,1)} %grads.1, ...), custom_call_target="tpu_custom_call" | custom-call | tf_op jit(solution)/shard_map/attend_both_ways/pallas_call | solution.py:468
  47.9 31.4 %reduce_and_return.1 = (bf16[16,4096]{1,0:T(8,128)(2,1)S(1)}, bf16[8,32,1024]{2,1,0:T(8,128)(2,1)S(1)}) custom-call(bf16[8,32,1024]{2,1,0:T(8,128)(2,1)S(1)} %get-tuple-element.20.grad_rows, s32[4,8,128]{2,1,0:T(8,128)S(1)} %get-tuple-element.21.facts, bf16[4096,512]{1,0:T(8,128)(2,1)} %bitcast.9, bf16[4096,512]{1,0:T(8,128)(2,1)} %bitcast.11), custom_call_target="tpu_custom_call" | custom-call | tf_op jit(solution)/shard_map/reduce_and_return/pallas_call | solution.py:484
  79.4 5.7 %weight_gradients.1 = (bf16[1,4096,512]{2,1,0:T(8,128)(2,1)}, bf16[1,4096,512]{2,1,0:T(8,128)(2,1)}) custom-call(bf16[256,4096]{1,0:T(8,128)(2,1)S(1)} %get-tuple-element.23.group, bf16[256,1024]{1,0:T(8,128)(2,1)S(1)} %bitcast.5), custom_call_target="tpu_custom_call" | custom-call | tf_op jit(solution)/shard_map/weight_gradients/pallas_call | solution.py:519
  85.1 0.7 copy.17
  (1 shorter events, 0.0 us)
Async XLA Ops:
  2.7 0.9 %copy-start.1 = (bf16[1,16,4096]{2,1,0:T(8,128)(2,1)S(1)}, bf16[1,16,4096]{2,1,0:T(8,128)(2,1)}, u32[]{:S(2)}) copy-start(bf16[1,16,4096]{2,1,0:T(8,128)(2,1)} %param.8) | copy-start | bytes 393220
  3.6 33.7 %copy-start = (bf16[1,2,128,4096]{3,2,1,0:T(8,128)(2,1)S(1)}, bf16[1,2,128,4096]{3,2,1,0:T(8,128)(2,1)}, u32[]{:S(2)}) copy-start(bf16[1,2,128,4096]{3,2,1,0:T(8,128)(2,1)} %queries.1) | copy-start | bytes 6291460

commit v5 on v4

--- a/solution.py
+++ b/solution.py
@@ -55,13 +55,76 @@
     return chosen
 
 
-def route_kernel(
+def attend(owners, lengths, queries, grads, rows_in, context, grad_queries, grad_rows):
+    slots, target_rows = queries.shape[:2]
+    head_cols = rows_in.shape[2] // 2
+    source_rows = rows_in.shape[1] // slots
+    heads = head_cols // HEAD
+    span = heads * source_rows
+    scaling = HEAD ** (-0.5)
+    same = (
+        lax.broadcasted_iota(jnp.int32, (span, head_cols), 0) // source_rows
+        == lax.broadcasted_iota(jnp.int32, (span, head_cols), 1) // HEAD
+    )
+    positions = lax.broadcasted_iota(jnp.int32, (heads, source_rows, target_rows), 1)
+    targets = lax.broadcasted_iota(jnp.int32, (target_rows, head_cols), 0)
+
+    def spread(rows):
+        wide = jnp.concatenate([rows] * heads, axis=0) if heads > 1 else rows
+        return jnp.where(same, wide.astype(F32), 0.0).astype(BF16)
+
+    def gather(wide):
+        return jnp.concatenate(
+            [
+                wide[h * source_rows : (h + 1) * source_rows, h * HEAD : (h + 1) * HEAD]
+                for h in range(heads)
+            ],
+            axis=1,
+        )
+
+    nt = (((1,), (1,)), ((), ()))
+    tn = (((0,), (0,)), ((), ()))
+    for owner, slot in [(owner, slot) for owner in owners for slot in range(slots)]:
+        lanes = pl.ds(pl.multiple_of(owner * head_cols, HEAD), head_cols)
+        near = slice(slot * source_rows, (slot + 1) * source_rows)
+        src = jnp.maximum(lengths[slot : slot + 1, 0:1], 1).reshape(1, 1, 1)
+        key_valid = positions < src
+        row_keep = targets < lengths[slots + slot : slots + slot + 1, 0:1]
+        q = queries[slot, :, lanes]
+        grad = jnp.where(row_keep, grads[slot, :, lanes].astype(F32), 0.0).astype(BF16)
+        keys = spread(rows_in[owner, near, :head_cols])
+        values = spread(rows_in[owner, near, head_cols:])
+        scores = lax.dot_general(keys, q, nt, preferred_element_type=F32) * scaling
+        scores = scores.reshape(heads, source_rows, target_rows)
+        scores = jnp.where(key_valid, scores, masked_score)
+        shifted = jnp.exp(scores - jnp.max(scores, axis=1, keepdims=True))
+        attention = shifted / jnp.sum(shifted, axis=1, keepdims=True)
+        attention_bf = attention.reshape(span, target_rows).astype(BF16)
+        out = lax.dot_general(attention_bf, values, tn, preferred_element_type=F32)
+        context[slot, :, lanes] = jnp.where(row_keep, out, 0.0).astype(BF16)
+        grad_values = jnp.dot(attention_bf, grad, preferred_element_type=F32)
+        grad_attention = lax.dot_general(values, grad, nt, preferred_element_type=F32)
+        grad_attention = grad_attention.reshape(heads, source_rows, target_rows)
+        row_dot = jnp.sum(attention * grad_attention, axis=1, keepdims=True)
+        grad_scores = attention * (grad_attention - row_dot)
+        grad_scores = grad_scores.reshape(span, target_rows).astype(BF16)
+        out = lax.dot_general(grad_scores, keys, tn, preferred_element_type=F32)
+        grad_queries[slot, :, lanes] = (out * scaling).astype(BF16)
+        grad_keys = jnp.dot(grad_scores, q, preferred_element_type=F32) * scaling
+        grad_rows[owner, near, :head_cols] = gather(grad_keys).astype(BF16)
+        grad_rows[owner, near, head_cols:] = gather(grad_values).astype(BF16)
+
+
+def whole_kernel(
     langs, shards, slots,
-    memory, facts_in, key_weight, value_weight,
-    group, rows_out, facts, lengths,
+    memory, facts_in, key_weight, value_weight, queries_in, grads_in,
+    group, context, grad_queries, grad_memory, all_rows,
+    facts, lengths, queries, grads, rows_in, grad_rows,
     column, weights, total, outgoing,
+    partial, first, paired, second, returning, third,
     weight_sem, fact_send, fact_recv, z_send, z_recv,
     p_send, p_recv, s_send, s_recv, a_send, a_recv,
+    b_send, b_recv, f_send, f_recv, q_send, q_recv, y_send, y_recv,
 ):
     lang = lax.axis_index("lang")
     shard = lax.axis_index("shard")
@@ -83,6 +146,12 @@
     ]
     for load in loads:
         load.start()
+    tensors = [
+        pltpu.make_async_copy(queries_in, queries, weight_sem.at[3]),
+        pltpu.make_async_copy(grads_in, grads, weight_sem.at[4]),
+    ]
+    for load in tensors:
+        load.start()
     enter(lang, shard, langs, shards)
 
     sent = []
@@ -120,11 +189,11 @@
     sent += fact_copies
     chosen = selection(facts, lang, langs, slots)
     for r in range(slots):
-        for row, first in ((1, 0), (2, slots)):
+        for row, base in ((1, 0), (2, slots)):
             value = jnp.zeros((1, 1), jnp.int32)
             for j in range(langs):
                 value = value + chosen[r][j] * facts[j, row : row + 1, 0:1]
-            lengths[first + r : first + r + 1, :] = jnp.broadcast_to(value, (1, 128))
+            lengths[base + r : base + r + 1, :] = jnp.broadcast_to(value, (1, 128))
     weigh = [[chosen[r][j].astype(F32) for j in range(langs)] for r in range(slots)]
 
     def window(who, c):
@@ -197,126 +266,55 @@
                 load.wait()
         if 0 <= turn - 2:
             project(turn - 2)
-    exchange(lang, shard, shards, outgoing, rows_out, a_send, a_recv)
-    for copy in sent:
-        copy.wait_send()
-
-
-def exchange(lang, shard, shards, outgoing, incoming, send_sem, recv_sem):
-    copies = []
-    for d in range(1, shards):
-        target = lax.rem(shard + d, shards)
-        copy = remote(
-            outgoing.at[target], incoming.at[shard], send_sem.at[d], recv_sem.at[d], (lang, target)
-        )
-        copy.start()
-        copies.append(copy)
-    incoming[shard] = outgoing[shard]
-    for copy in copies:
-        copy.wait_recv()
-    for copy in copies:
-        copy.wait_send()
-
-
-def attend_kernel(lengths, queries, grads, rows_in, context, grad_queries, grad_rows):
-    slot = pl.program_id(0)
-    groups = rows_in.shape[0]
-    source_rows = rows_in.shape[1]
-    head_cols = rows_in.shape[2] // 2
-    target_rows = queries.shape[2]
-    heads = head_cols // HEAD
-    span = heads * source_rows
-    scaling = HEAD ** (-0.5)
-    slots = pl.num_programs(0)
-    src = lengths[pl.ds(slot, 1), :]
-    tgt = lengths[pl.ds(slots + slot, 1), :]
-    src = jnp.maximum(src, 1)[:, 0:1].reshape(1, 1, 1)
-    tgt = tgt[:, 0:1]
-    key_valid = lax.broadcasted_iota(jnp.int32, (heads, source_rows, target_rows), 1) < src
-    row_keep = lax.broadcasted_iota(jnp.int32, (target_rows, head_cols), 0) < tgt
-    same = (
-        lax.broadcasted_iota(jnp.int32, (span, head_cols), 0) // source_rows
-        == lax.broadcasted_iota(jnp.int32, (span, head_cols), 1) // HEAD
-    )
-
-    def spread(rows):
-        wide = jnp.concatenate([rows] * heads, axis=0) if heads > 1 else rows
-        return jnp.where(same, wide.astype(F32), 0.0).astype(BF16)
-
-    def gather(wide):
-        return jnp.concatenate(
-            [
-                wide[h * source_rows : (h + 1) * source_rows, h * HEAD : (h + 1) * HEAD]
-                for h in range(heads)
-            ],
-            axis=1,
-        )
-
+
+    def bring(d):
+        return remote(
+            outgoing.at[lax.rem(shard + d, shards)], rows_in.at[shard],
+            a_send.at[d], a_recv.at[d], (lang, lax.rem(shard + d, shards)),
+        )
+
+    def give(d):
+        owner = lax.rem(shard + shards - d, shards)
+        return remote(
+            grad_rows.at[owner], all_rows.at[shard], b_send.at[d], b_recv.at[d], (lang, owner)
+        )
+
+    def start_bring(d, carry):
+        bring(d).start()
+        return carry
+
+    def end_bring(d, carry):
+        bring(d).wait_send()
+        return carry
+
+    def end_give(d, carry):
+        give(d).wait_recv()
+        give(d).wait_send()
+        return carry
+
+    lax.fori_loop(1, shards, start_bring, 0)
+    rows_in[shard] = outgoing[shard]
+    for load in tensors:
+        load.wait()
+    state = (lengths, queries, grads, rows_in, context, grad_queries, grad_rows)
+
+    def attend_pair(step, carry):
+        for d in (2 * step, 2 * step + 1):
+            bring(d).wait_recv()
+        attend([lax.rem(shard + shards - d, shards) for d in (2 * step, 2 * step + 1)], *state)
+        for d in (2 * step, 2 * step + 1):
+            give(d).start()
+        return carry
+
+    bring(1).wait_recv()
+    attend([shard, lax.rem(shard + shards - 1, shards)], *state)
+    give(1).start()
+    all_rows[shard] = grad_rows[shard]
+    lax.fori_loop(1, shards // 2, attend_pair, 0)
+    lax.fori_loop(1, shards, end_give, 0)
+    lax.fori_loop(1, shards, end_bring, 0)
     nt = (((1,), (1,)), ((), ()))
-    tn = (((0,), (0,)), ((), ()))
-    for g in range(groups):
-        lanes = slice(g * head_cols, (g + 1) * head_cols)
-        q = queries[0, 0, :, lanes]
-        grad = jnp.where(row_keep, grads[0, 0, :, lanes].astype(F32), 0.0).astype(BF16)
-        keys = spread(rows_in[g, :, :head_cols])
-        values = spread(rows_in[g, :, head_cols:])
-        scores = lax.dot_general(keys, q, nt, preferred_element_type=F32) * scaling
-        scores = scores.reshape(heads, source_rows, target_rows)
-        scores = jnp.where(key_valid, scores, masked_score)
-        shifted = jnp.exp(scores - jnp.max(scores, axis=1, keepdims=True))
-        attention = shifted / jnp.sum(shifted, axis=1, keepdims=True)
-        attention_bf = attention.reshape(span, target_rows).astype(BF16)
-        out = lax.dot_general(attention_bf, values, tn, preferred_element_type=F32)
-        context[0, 0, :, lanes] = jnp.where(row_keep, out, 0.0).astype(BF16)
-        grad_values = jnp.dot(attention_bf, grad, preferred_element_type=F32)
-        grad_attention = lax.dot_general(values, grad, nt, preferred_element_type=F32)
-        grad_attention = grad_attention.reshape(heads, source_rows, target_rows)
-        row_dot = jnp.sum(attention * grad_attention, axis=1, keepdims=True)
-        grad_scores = attention * (grad_attention - row_dot)
-        grad_scores = grad_scores.reshape(span, target_rows).astype(BF16)
-        out = lax.dot_general(grad_scores, keys, tn, preferred_element_type=F32)
-        grad_queries[0, 0, :, lanes] = (out * scaling).astype(BF16)
-        grad_keys = jnp.dot(grad_scores, q, preferred_element_type=F32) * scaling
-        grad_rows[g, :, :head_cols] = gather(grad_keys).astype(BF16)
-        grad_rows[g, :, head_cols:] = gather(grad_values).astype(BF16)
-
-
-def reduce_kernel(
-    langs, shards, slots,
-    grad_rows, facts, key_weight, value_weight,
-    grad_memory, all_rows,
-    weights, partial, first, paired, second, returning, third,
-    weight_sem, a_send, a_recv, f_send, f_recv, p_send, p_recv, z_send, z_recv,
-):
-    lang = lax.axis_index("lang")
-    shard = lax.axis_index("shard")
-    core = lax.rem(shard, 2)
-    chip = shard // 2
-    chips = shards // 2
-    sibling = (lang, chip * 2 + 1 - core)
-    rows = grad_memory.shape[0]
-    cols = grad_memory.shape[1] // CHUNKS
-    head_cols = key_weight.shape[1]
-    block = slots * rows
-    nt = (((1,), (1,)), ((), ()))
-
-    loads = [
-        pltpu.make_async_copy(key_weight, weights.at[:, 0:head_cols], weight_sem.at[0]),
-        pltpu.make_async_copy(
-            value_weight, weights.at[:, head_cols : 2 * head_cols], weight_sem.at[1]
-        ),
-    ]
-    for load in loads:
-        load.start()
-    enter(lang, shard, langs, shards)
-    exchange(lang, shard, shards, grad_rows, all_rows, a_send, a_recv)
-    for load in loads:
-        load.wait()
-
-    sent = []
     f_copies = []
-    chosen = selection(facts, lang, langs, slots)
-    weigh = [[chosen[r][j].astype(F32) for j in range(langs)] for r in range(slots)]
 
     def project_back(c):
         product = lax.dot_general(
@@ -345,7 +343,7 @@
             pair = partial[c, core, other].astype(F32) + first[c, other].astype(F32)
             paired[c, d] = pair.astype(BF16)
             copy = remote(
-                paired.at[c, d], second.at[c, d], p_send.at[c, d], p_recv.at[c, d],
+                paired.at[c, d], second.at[c, d], q_send.at[c, d], q_recv.at[c, d],
                 (lang, other * 2 + core),
             )
             copy.start()
@@ -367,7 +365,7 @@
         for d in range(1, langs):
             other = lax.rem(lang + d, langs)
             copy = remote(
-                returning.at[c, other], third.at[c, d], z_send.at[c, d], z_recv.at[c, d],
+                returning.at[c, other], third.at[c, d], y_send.at[c, d], y_recv.at[c, d],
                 (other, shard),
             )
             copy.start()
@@ -426,22 +424,41 @@
     facts_in = jnp.concatenate([lang_id, src_len, tgt_len, jnp.zeros((5,), jnp.int32)])
     facts_in = jnp.broadcast_to(facts_in[:, None], (8, 128))
 
-    group, rows_in, facts, lengths = pl.pallas_call(
-        functools.partial(route_kernel, langs, shards, slots),
+    three = jax.ShapeDtypeStruct((shards, block, 2 * head_cols), BF16)
+    tensor = jax.ShapeDtypeStruct(queries.shape[1:], BF16)
+    three_vmem = pltpu.VMEM(three.shape, BF16)
+    tensor_vmem = pltpu.VMEM(tensor.shape, BF16)
+    pairs_vmem = pltpu.VMEM((CHUNKS, chips, block, cols), BF16)
+    back_vmem = pltpu.VMEM((CHUNKS, langs, rows, cols), BF16)
+    group, context, grad_queries, grad_memory, all_rows = pl.pallas_call(
+        functools.partial(whole_kernel, langs, shards, slots),
         out_shape=(
             jax.ShapeDtypeStruct((total_rows, width), BF16),
-            jax.ShapeDtypeStruct((shards, block, 2 * head_cols), BF16),
-            jax.ShapeDtypeStruct((langs, 8, 128), jnp.int32),
-            jax.ShapeDtypeStruct((2 * slots, 128), jnp.int32),
+            tensor,
+            tensor,
+            jax.ShapeDtypeStruct((rows, width), BF16),
+            three,
         ),
-        in_specs=[hbm, vmem, hbm, hbm],
-        out_specs=(vmem, vmem, vmem, vmem),
+        in_specs=[hbm, vmem, hbm, hbm, hbm, hbm],
+        out_specs=(vmem, vmem, vmem, vmem, vmem),
         scratch_shapes=[
+            pltpu.VMEM((langs, 8, 128), jnp.int32),
+            pltpu.VMEM((2 * slots, 128), jnp.int32),
+            tensor_vmem,
+            tensor_vmem,
+            three_vmem,
+            three_vmem,
             pltpu.VMEM((langs, rows, width), BF16),
             pltpu.VMEM((width, 2 * head_cols), BF16),
             pltpu.VMEM((total_rows, 2 * head_cols), F32),
-            pltpu.VMEM((shards, block, 2 * head_cols), BF16),
-            dma((3,)),
+            three_vmem,
+            pltpu.VMEM((CHUNKS, 2, chips, block, cols), BF16),
+            pairs_vmem,
+            pairs_vmem,
+            pairs_vmem,
+            back_vmem,
+            back_vmem,
+            dma((5,)),
             dma((langs,)),
             dma((langs,)),
             dma((langs, CHUNKS)),
@@ -452,52 +469,6 @@
             dma((chips, CHUNKS)),
             dma((shards,)),
             dma((shards,)),
-        ],
-        compiler_params=pltpu.CompilerParams(
-            collective_id=0, has_side_effects=True, vmem_limit_bytes=VMEM_BYTES
-        ),
-        name="route_and_project",
-    )(memory[0], facts_in, keys, values)
-
-    per_step = max(1, min(shards, 2048 // head_cols))
-    steps = shards // per_step
-    wide = pl.BlockSpec(
-        (1, 1, target_rows, per_step * head_cols), lambda r, p: (0, r, 0, p)
-    )
-    narrow = pl.BlockSpec((per_step, rows, 2 * head_cols), lambda r, p: (p, r, 0))
-    context, grad_queries, grad_rows = pl.pallas_call(
-        attend_kernel,
-        grid=(slots, steps),
-        out_shape=(
-            jax.ShapeDtypeStruct(queries.shape, BF16),
-            jax.ShapeDtypeStruct(queries.shape, BF16),
-            jax.ShapeDtypeStruct(rows_in.shape, BF16),
-        ),
-        in_specs=[
-            pl.BlockSpec((2 * slots, 128), lambda r, p: (0, 0)), wide, wide, narrow
-        ],
-        out_specs=(wide, wide, narrow),
-        compiler_params=pltpu.CompilerParams(vmem_limit_bytes=VMEM_BYTES),
-        name="attend_both_ways",
-    )(lengths, queries, grad_context, rows_in)
-
-    grad_memory, all_rows = pl.pallas_call(
-        functools.partial(reduce_kernel, langs, shards, slots),
-        out_shape=(
-            jax.ShapeDtypeStruct((rows, width), BF16),
-            jax.ShapeDtypeStruct((shards, block, 2 * head_cols), BF16),
-        ),
-        in_specs=[vmem, vmem, hbm, hbm],
-        out_specs=(vmem, vmem),
-        scratch_shapes=[
-            pltpu.VMEM((width, 2 * head_cols), BF16),
-            pltpu.VMEM((CHUNKS, 2, chips, block, cols), BF16),
-            pltpu.VMEM((CHUNKS, chips, block, cols), BF16),
-            pltpu.VMEM((CHUNKS, chips, block, cols), BF16),
-            pltpu.VMEM((CHUNKS, chips, block, cols), BF16),
-            pltpu.VMEM((CHUNKS, langs, rows, cols), BF16),
-            pltpu.VMEM((CHUNKS, langs, rows, cols), BF16),
-            dma((2,)),
             dma((shards,)),
             dma((shards,)),
             dma((CHUNKS,)),
@@ -508,10 +479,10 @@
             dma((CHUNKS, langs)),
         ],
         compiler_params=pltpu.CompilerParams(
-            collective_id=1, has_side_effects=True, vmem_limit_bytes=VMEM_BYTES
+            collective_id=0, has_side_effects=True, vmem_limit_bytes=VMEM_BYTES
         ),
-        name="reduce_and_return",
-    )(grad_rows, facts, keys, values)
+        name="route_attend_reduce",
+    )(memory[0], facts_in, keys, values, queries[0], grad_context[0])
 
     flat = all_rows.reshape(total_rows, 2 * head_cols)
     tile = width // 8
@@ -532,8 +503,8 @@
         name="weight_gradients",
     )(group, flat)
     return (
-        context,
-        grad_queries,
+        context[None],
+        grad_queries[None],
         grad_memory[None],
         grad_key,
         grad_value,

time: 85.9 us -> 81.5 us (0.949)
  Pallas kernels: 81.4 us -> 73.3 us
  local copies, waits for them, and re-layouts: 1.64 us -> 5.31 us
    pallas_call x3 -> x1, Pallas kernels: 75.7 us -> 67.5 us  [local(): pl.pallas_call(functools.partial(whole_kernel, langs, shards, slots), out...]
    unnamed x5 -> x9, local copies, waits for them, and re-layouts: 1.56 us -> 5.23 us
where the time goes in v5:
time: 81.5 us; the launch traced here: 81.3 us
  Pallas kernels  73.3 us (90%)
  local copies, waits for them, and re-layouts  5.31 us (7%)
  between operations  2.6 us (3%)
    pallas_call x1, Pallas kernels, local(): pl.pallas_call(functools.partial(whole_kernel, langs, shards, slots), out...  67.5 us
    pallas_call x1, Pallas kernels, local(): pl.pallas_call(weight_kernel, grid=(8,), out_shape=(jax.ShapeDtypeStruct(...  5.82 us
    unnamed x9, local copies, waits for them, and re-layouts  5.23 us

profile of v5, /device:TPU:0, one launch (start us, length us, event | category | flops | bytes accessed | tf_op | source)
XLA Modules:
  0.0 81.3 jit_solution(13781575628075621570)
XLA Ops:
  2.6 0.1 pad_add_fusion
  2.7 0.1 broadcast_in_dim.15.facts_in
  2.7 0.0 copy-start
  2.7 0.9 %copy-done = bf16[1,16,4096]{2,1,0:T(8,128)(2,1)S(1)} copy-done((bf16[1,16,4096]{2,1,0:T(8,128)(2,1)S(1)}, bf16[1,16,4096]{2,1,0:T(8,128)(2,1)}, u32[]{:S(2)}) %copy-start) | copy-done | bytes 131096
  3.6 67.5 %route_attend_reduce.1 = (bf16[256,4096]{1,0:T(8,128)(2,1)S(1)}, bf16[2,128,4096]{2,1,0:T(8,128)(2,1)}, bf16[2,128,4096]{2,1,0:T(8,128)(2,1)}, bf16[16,4096]{1,0:T(8,128)(2,1)S(1)}, bf16[8,32,1024]{2,1,0:T(8,128)(2,1)S(1)}) custom-call(bf16[16,4096]{1,0:T(8,128)(2,1)S(1)} %bitcast.10, s32[8,128]{1,0:T(8,128)S(1)} %broadcast_in_dim.15.facts_in, ...), custom_call_target="tpu_custom_call" | custom-call | tf_op jit(solution)/shard_map/route_attend_reduce/pallas_call | solution.py:433
  71.2 0.0 copy-start.2
  71.2 5.8 %weight_gradients.1 = (bf16[1,4096,512]{2,1,0:T(8,128)(2,1)}, bf16[1,4096,512]{2,1,0:T(8,128)(2,1)}) custom-call(bf16[256,4096]{1,0:T(8,128)(2,1)S(1)} %get-tuple-element.15.group, bf16[256,1024]{1,0:T(8,128)(2,1)S(1)} %bitcast.9), custom_call_target="tpu_custom_call" | custom-call | tf_op jit(solution)/shard_map/weight_gradients/pallas_call | solution.py:490
  77.0 0.0 copy-done.2
  77.0 0.0 copy-start.1
  77.0 1.3 %copy.19 = bf16[1,2,128,4096]{3,2,1,0:T(8,128)(2,1)} copy(bf16[1,2,128,4096]{3,2,1,0:T(8,128)(2,1)S(1)} %bitcast.15) | data formatting | bytes 4194304
  78.3 1.0 %copy-done.1 = bf16[2,128,4096]{2,1,0:T(8,128)(2,1)S(1)} copy-done((bf16[2,128,4096]{2,1,0:T(8,128)(2,1)S(1)}, bf16[2,128,4096]{2,1,0:T(8,128)(2,1)}, u32[]{:S(2)}) %copy-start.1) | copy-done | bytes 2097176
  79.3 1.3 %copy.20 = bf16[1,2,128,4096]{3,2,1,0:T(8,128)(2,1)} copy(bf16[1,2,128,4096]{3,2,1,0:T(8,128)(2,1)S(1)} %bitcast.14) | data formatting | bytes 4194304
  80.7 0.7 copy.21
  (1 shorter events, 0.0 us)
Async XLA Ops:
  2.7 0.9 %copy-start = (bf16[1,16,4096]{2,1,0:T(8,128)(2,1)S(1)}, bf16[1,16,4096]{2,1,0:T(8,128)(2,1)}, u32[]{:S(2)}) copy-start(bf16[1,16,4096]{2,1,0:T(8,128)(2,1)} %param.8) | copy-start | bytes 393220
  71.2 5.8 %copy-start.2 = (bf16[2,128,4096]{2,1,0:T(8,128)(2,1)S(1)}, bf16[2,128,4096]{2,1,0:T(8,128)(2,1)}, u32[]{:S(2)}) copy-start(bf16[2,128,4096]{2,1,0:T(8,128)(2,1)} %get-tuple-element.12) | copy-start | bytes 6291460
  77.0 2.3 %copy-start.1 = (bf16[2,128,4096]{2,1,0:T(8,128)(2,1)S(1)}, bf16[2,128,4096]{2,1,0:T(8,128)(2,1)}, u32[]{:S(2)}) copy-start(bf16[2,128,4096]{2,1,0:T(8,128)(2,1)} %get-tuple-element.13) | copy-start | bytes 6291460

commit v6 on v5

--- a/solution.py
+++ b/solution.py
@@ -395,7 +395,13 @@
         copy.wait_send()
 
 
-def weight_kernel(group, grads, grad_key, grad_value):
+def weight_kernel(
+    group, grads, context_in, queries_in, memory_in,
+    grad_key, grad_value, context, grad_queries, grad_memory,
+):
+    context[...] = context_in[...]
+    grad_queries[...] = queries_in[...]
+    grad_memory[...] = memory_in[...]
     head_cols = grad_key.shape[2]
     product = lax.dot_general(
         group[...], grads[...], (((0,), (0,)), ((), ())), preferred_element_type=F32
@@ -487,21 +493,29 @@
     flat = all_rows.reshape(total_rows, 2 * head_cols)
     tile = width // 8
     out_tile = pl.BlockSpec((1, tile, head_cols), lambda i: (0, i, 0))
-    grad_key, grad_value = pl.pallas_call(
+    tensor_tile = pl.BlockSpec((slots, target_rows, tile), lambda i: (0, 0, i))
+    memory_tile = pl.BlockSpec((rows, tile), lambda i: (0, i))
+    grad_key, grad_value, context, grad_queries, grad_memory = pl.pallas_call(
         weight_kernel,
         grid=(8,),
         out_shape=(
             jax.ShapeDtypeStruct(key_weight.shape, BF16),
             jax.ShapeDtypeStruct(value_weight.shape, BF16),
+            tensor,
+            tensor,
+            jax.ShapeDtypeStruct((rows, width), BF16),
         ),
         in_specs=[
             pl.BlockSpec((total_rows, tile), lambda i: (0, i)),
             pl.BlockSpec((total_rows, 2 * head_cols), lambda i: (0, 0)),
+            tensor_tile,
+            tensor_tile,
+            memory_tile,
         ],
-        out_specs=(out_tile, out_tile),
+        out_specs=(out_tile, out_tile, tensor_tile, tensor_tile, memory_tile),
         compiler_params=pltpu.CompilerParams(vmem_limit_bytes=VMEM_BYTES),
         name="weight_gradients",
-    )(group, flat)
+    )(group, flat, context, grad_queries, grad_memory)
     return (
         context[None],
         grad_queries[None],

time: 81.5 us -> 81 us (level)
  local copies, waits for them, and re-layouts: 5.31 us -> 0.98 us
  Pallas kernels: 73.3 us -> 77 us
    unnamed x9 -> x2, local copies, waits for them, and re-layouts: 5.23 us -> 0.91 us
    pallas_call x1, Pallas kernels: 5.82 us -> 9.46 us  [local(): pl.pallas_call(weight_kernel, grid=(8,), out_shape=(jax.ShapeDtypeStruct(...]
where the time goes in v6:
time: 81 us; the launch traced here: 80.6 us
  Pallas kernels  77 us (95%)
  between operations  2.59 us (3%)
  local copies, waits for them, and re-layouts  0.98 us (1%)
    pallas_call x1, Pallas kernels, local(): pl.pallas_call(functools.partial(whole_kernel, langs, shards, slots), out...  67.5 us
    pallas_call x1, Pallas kernels, local(): pl.pallas_call(weight_kernel, grid=(8,), out_shape=(jax.ShapeDtypeStruct(...  9.46 us

profile of v6, /device:TPU:0, one launch (start us, length us, event | category | flops | bytes accessed | tf_op | source)
XLA Modules:
  0.0 80.6 jit_solution(9734812488548571106)
XLA Ops:
  2.6 0.1 pad_add_fusion
  2.7 0.1 broadcast_in_dim.15.facts_in
  2.7 0.0 copy-start
  2.7 0.9 %copy-done = bf16[1,16,4096]{2,1,0:T(8,128)(2,1)S(1)} copy-done((bf16[1,16,4096]{2,1,0:T(8,128)(2,1)S(1)}, bf16[1,16,4096]{2,1,0:T(8,128)(2,1)}, u32[]{:S(2)}) %copy-start) | copy-done | bytes 131096
  3.6 67.5 %route_attend_reduce.1 = (bf16[256,4096]{1,0:T(8,128)(2,1)S(1)}, bf16[2,128,4096]{2,1,0:T(8,128)(2,1)}, bf16[2,128,4096]{2,1,0:T(8,128)(2,1)}, bf16[16,4096]{1,0:T(8,128)(2,1)S(1)}, bf16[8,32,1024]{2,1,0:T(8,128)(2,1)S(1)}) custom-call(bf16[16,4096]{1,0:T(8,128)(2,1)S(1)} %bitcast.10, s32[8,128]{1,0:T(8,128)S(1)} %broadcast_in_dim.15.facts_in, ...), custom_call_target="tpu_custom_call" | custom-call | tf_op jit(solution)/shard_map/route_attend_reduce/pallas_call | solution.py:439
  71.1 9.5 %weight_gradients.1 = (bf16[1,4096,512]{2,1,0:T(8,128)(2,1)}, bf16[1,4096,512]{2,1,0:T(8,128)(2,1)}, bf16[2,128,4096]{2,1,0:T(8,128)(2,1)}, bf16[2,128,4096]{2,1,0:T(8,128)(2,1)}, bf16[16,4096]{1,0:T(8,128)(2,1)}) custom-call(bf16[256,4096]{1,0:T(8,128)(2,1)S(1)} %get-tuple-element.15.group, bf16[256,1024]{1,0:T(8,128)(2,1)S(1)} %bitcast.9, ...), custom_call_target="tpu_custom_call" | custom-call | tf_op jit(solution)/shard_map/weight_gradients/pallas_call | solution.py:498
  (1 shorter events, 0.0 us)
Async XLA Ops:
  2.7 0.9 %copy-start = (bf16[1,16,4096]{2,1,0:T(8,128)(2,1)S(1)}, bf16[1,16,4096]{2,1,0:T(8,128)(2,1)}, u32[]{:S(2)}) copy-start(bf16[1,16,4096]{2,1,0:T(8,128)(2,1)} %param.8) | copy-start | bytes 393220
